TPU v7x, 128 devices: a whole 4x4x4 slice. The times are simulated.
128 devices in a mesh: dp: 8 (over y, z_hi), ctx: 16 (over x, z_lo, core).
Axes of the slice: x: 4, y: 4, z: 4 (z_hi: 2, z_lo: 2; z = z_hi * 2 + z_lo), core: 2. Of those that a mesh axis runs over, the one named last changes fastest.
Arguments:
- queries: bfloat16 [8, 4096, 2048], P('dp', 'ctx'), may hold values from -6 to 6
- keys: bfloat16 [8, 4096, 2048], P('dp', 'ctx'), may hold values from -6 to 6
- values: bfloat16 [8, 4096, 2048], P('dp', 'ctx'), may hold values from -6 to 6
- out_grad: bfloat16 [8, 4096, 2048], P('dp', 'ctx'), may hold values from -96 to 96
- layer_input: bfloat16 [8, 4096, 2048], P('dp', 'ctx'), may hold values from -6 to 6
- global_blocks: int32 [8, 2], P('dp'), may hold values from 0 to 31, as said below
- random_blocks: int32 [8, 32, 3], P('dp'), may hold values from 0 to 31, as said below
Outputs:
- query_grad: bfloat16 [8, 4096, 2048], P('dp', 'ctx')
- key_grad: bfloat16 [8, 4096, 2048], P('dp', 'ctx')
- value_grad: bfloat16 [8, 4096, 2048], P('dp', 'ctx')
- value_weight_grad: float32 [2048, 2048], P(('dp', 'ctx'))
Inputs may be any that keep to these rules, and one draw needn't show every extreme that they name: `global_blocks`: for each document, 2 distinct blocks. `random_blocks`: for each document and query block b, 3 distinct blocks, none of them b-1, b, b+1 or a global block of that document.
All inputs are finite; a program needn't handle non-finite values.
Results may differ from a plain program's by a relative error of at most 0.018.
Values may be sent and summed in bfloat16 or wider, within the bound.
No kernel may reach another device: no remote copies, remote signals or barrier semaphores. Data moves between devices by JAX's collectives and lax.ppermute only.
A program may use at most 128 MiB of HBM per device.

v0:
```python
import math

import jax
import jax.numpy as jnp
from jax import lax
from jax.sharding import PartitionSpec as P

HEAD_DIM = 128
BLOCK = 128


def block_table(global_row, random_rows, block_count):
    blocks = jnp.arange(block_count, dtype=jnp.int32)
    left_side = blocks - 1
    right_side = blocks + 1
    global_wide = jnp.broadcast_to(global_row[None, :], (block_count, global_row.shape[0]))
    table = jnp.concatenate(
        [left_side[:, None], blocks[:, None], right_side[:, None], global_wide, random_rows], axis=1
    )
    counted = jnp.concatenate(
        [
            (left_side >= 0)[:, None],
            jnp.ones((block_count, 1), jnp.bool_),
            (right_side < block_count)[:, None],
            jnp.abs(global_wide - blocks[:, None]) > 1,
            jnp.ones(random_rows.shape, jnp.bool_),
        ],
        axis=1,
    )
    return (jnp.clip(table, 0, block_count - 1), counted)


def group_probs(query_tile, key_tile, counted_tile, scale):
    scores = (
        jnp.einsum("gihe,gjkhe->ghijk", query_tile, key_tile, preferred_element_type=jnp.float32)
        * scale
    )
    scores = jnp.where(counted_tile[:, None, None, :, None], scores, -jnp.inf)
    largest = jnp.max(scores, axis=(3, 4), keepdims=True)
    weights = jnp.exp(scores - largest)
    probs = weights / jnp.sum(weights, axis=(3, 4), keepdims=True)
    return (probs, probs.astype(jnp.bfloat16))


def group_output(probs_low, value_tile):
    return jnp.einsum(
        "ghijk,gjkhe->gihe", probs_low, value_tile, preferred_element_type=jnp.float32
    )


def group_grads(probs, probs_low, query_tile, key_tile, value_tile, grad_tile, delta, scale):
    value_part = jnp.einsum(
        "ghijk,gihe->gjkhe", probs_low, grad_tile, preferred_element_type=jnp.float32
    )
    dprobs = jnp.einsum(
        "gihe,gjkhe->ghijk", grad_tile, value_tile, preferred_element_type=jnp.float32
    )
    centered = dprobs - jnp.transpose(delta, (0, 2, 1))[:, :, :, None, None]
    dscore = (probs * centered * scale).astype(jnp.bfloat16)
    query_part = jnp.einsum(
        "ghijk,gjkhe->gihe", dscore, key_tile, preferred_element_type=jnp.float32
    ).astype(jnp.bfloat16)
    key_part = jnp.einsum(
        "ghijk,gihe->gjkhe", dscore, query_tile, preferred_element_type=jnp.float32
    )
    return (query_part, key_part, value_part)


def step_layout(query4):
    block_count = query4.shape[0]
    per_step = min(block_count, max(1, 512 // query4.shape[1]))
    return (per_step, block_count // per_step, 1.0 / math.sqrt(query4.shape[3]))


def sparse_sweep(query4, key4, value4, grad4, table, counted):
    per_step, step_count, scale = step_layout(query4)

    def advance(carry, index):
        key_acc, value_acc = carry
        first = index * per_step
        query_tile = lax.dynamic_slice_in_dim(query4, first, per_step, 0)
        grad_tile = lax.dynamic_slice_in_dim(grad4, first, per_step, 0)
        picks = lax.dynamic_slice_in_dim(table, first, per_step, 0)
        counted_tile = lax.dynamic_slice_in_dim(counted, first, per_step, 0)
        key_tile = key4[picks]
        value_tile = value4[picks]
        probs, probs_low = group_probs(query_tile, key_tile, counted_tile, scale)
        attn_out = group_output(probs_low, value_tile)
        delta = jnp.sum(grad_tile.astype(jnp.float32) * attn_out, axis=-1)
        query_part, key_part, value_part = group_grads(
            probs, probs_low, query_tile, key_tile, value_tile, grad_tile, delta, scale
        )
        return ((key_acc.at[picks].add(key_part), value_acc.at[picks].add(value_part)), query_part)

    zeros = jnp.zeros(query4.shape, jnp.float32)
    (key_acc, value_acc), query_parts = lax.scan(
        advance, (zeros, zeros), jnp.arange(step_count, dtype=jnp.int32)
    )
    return (
        query_parts.reshape(query4.shape),
        key_acc.astype(jnp.bfloat16),
        value_acc.astype(jnp.bfloat16),
    )


def per_device(queries, keys, values, out_grad, layer_input, global_blocks, random_blocks):
    query_rows = queries[0]
    key_rows = keys[0]
    value_rows = values[0]
    grad_rows = out_grad[0]
    local_tokens = query_rows.shape[0]
    ctx_count = lax.axis_size("ctx")
    dp_count = lax.axis_size("dp")
    head_cols = query_rows.shape[1] // ctx_count
    doc_tokens = local_tokens * ctx_count
    block_count = doc_tokens // BLOCK
    shape4 = (block_count, BLOCK, head_cols // HEAD_DIM, HEAD_DIM)
    table, counted = block_table(global_blocks[0], random_blocks[0], block_count)
    query_heads, key_heads, value_heads, grad_heads = (
        lax.all_to_all(query_rows, "ctx", split_axis=1, concat_axis=0, tiled=True),
        lax.all_to_all(key_rows, "ctx", split_axis=1, concat_axis=0, tiled=True),
        lax.all_to_all(value_rows, "ctx", split_axis=1, concat_axis=0, tiled=True),
        lax.all_to_all(grad_rows, "ctx", split_axis=1, concat_axis=0, tiled=True),
    )
    query_part, key_part, value_part = sparse_sweep(
        query_heads.reshape(shape4),
        key_heads.reshape(shape4),
        value_heads.reshape(shape4),
        grad_heads.reshape(shape4),
        table,
        counted,
    )
    query_back, key_back, value_back = (
        lax.all_to_all(
            query_part.reshape(doc_tokens, head_cols),
            "ctx",
            split_axis=0,
            concat_axis=1,
            tiled=True,
        ),
        lax.all_to_all(
            key_part.reshape(doc_tokens, head_cols), "ctx", split_axis=0, concat_axis=1, tiled=True
        ),
        lax.all_to_all(
            value_part.reshape(doc_tokens, head_cols),
            "ctx",
            split_axis=0,
            concat_axis=1,
            tiled=True,
        ),
    )
    features = layer_input[0]
    weight_scale = 1.0 / math.sqrt(local_tokens * ctx_count * dp_count)
    weight_rows = lax.psum_scatter(
        lax.dot_general(
            features, value_back, (((0,), (0,)), ((), ())), preferred_element_type=jnp.float32
        )
        * weight_scale,
        ("dp", "ctx"),
        scatter_dimension=0,
        tiled=True,
    )
    return (query_back[None], key_back[None], value_back[None], weight_rows)


def solution(mesh):
    placed = (
        P("dp", "ctx", None),
        P("dp", "ctx", None),
        P("dp", "ctx", None),
        P("dp", "ctx", None),
        P("dp", "ctx", None),
        P("dp", None),
        P("dp", None, None),
    )
    return jax.shard_map(
        per_device,
        mesh=mesh,
        in_specs=placed,
        out_specs=(
            P("dp", "ctx", None),
            P("dp", "ctx", None),
            P("dp", "ctx", None),
            P(("dp", "ctx"), None),
        ),
        check_vma=False,
    )
```

profile of v0, /device:TPU:1, one launch (start us, length us, event | category | flops | bytes accessed | tf_op | source)
XLA Modules:
  0.0 1080.7 jit_solution(12265178307780225551)
XLA Ops:
  9.6 7.2 all-to-all-start.1
  18.1 14.4 %all-to-all-done.1 = bf16[256,16,128]{0,2,1:T(8,128)(2,1)S(1)} async-done(((bf16[256,16,128]{0,2,1:T(8,128)(2,1)}), bf16[256,16,128]{0,2,1:T(8,128)(2,1)S(1)}, u32[]{:S(2)}, u32[]{:S(2)}) %all-to-all-start.1) | async-done | bytes 1048608 | tf_op jit(solution)/shard_map/all_to_all | solution.py:121
  39.1 13.5 %all-to-all-done.3 = bf16[256,16,128]{0,2,1:T(8,128)(2,1)S(1)} async-done(((bf16[256,16,128]{0,2,1:T(8,128)(2,1)}), bf16[256,16,128]{0,2,1:T(8,128)(2,1)S(1)}, u32[]{:S(2)}, u32[]{:S(2)}) %all-to-all-start.3) | async-done | bytes 1048608 | tf_op jit(solution)/shard_map/all_to_all | solution.py:122
  60.3 13.2 %all-to-all-done.2 = bf16[256,16,128]{0,2,1:T(8,128)(2,1)} async-done(((bf16[256,16,128]{0,2,1:T(8,128)(2,1)}), bf16[256,16,128]{0,2,1:T(8,128)(2,1)}, u32[]{:S(2)}, u32[]{:S(2)}) %all-to-all-start.2) | async-done | bytes 1048608 | tf_op jit(solution)/shard_map/all_to_all | solution.py:123
  83.8 10.5 all-to-all-done
  97.4 261.9 %while.14 = (s32[]{:T(128)}, f32[32,128,1,128]{3,1,0,2:T(8,128)}, f32[32,128,1,128]{3,1,0,2:T(8,128)}, bf16[8,4,128,1,128]{4,2,1,0,3:T(8,128)(2,1)}, s32[8]{0:T(...) while((s32[]{:T(128)}, f32[32,128,1,128]{3,1,0,2:T(8,128)}, ...), condition=%wide.region_6.7_spmd, body=%wide.region_0.6_spmd.sunk | while | flops 819723904 | bytes 53243492 | solution.py:96
  124.0 6.2 scatter_fusion
  144.8 6.2 scatter_fusion.1
  156.8 6.1 scatter_fusion
  210.2 6.2 scatter_fusion.1
  222.2 6.1 scatter_fusion
  242.9 6.2 scatter_fusion.1
  254.9 6.2 scatter_fusion
  275.7 6.2 scatter_fusion.1
  287.7 6.2 scatter_fusion
  308.5 6.2 scatter_fusion.1
  320.5 6.1 scatter_fusion
  353.2 6.1 scatter_fusion
  361.1 18.9 %all_to_all.115 = bf16[16,256,128]{2,1,0:T(8,128)(2,1)S(1)} all-to-all(bf16[16,256,128]{2,1,0:T(8,128)(2,1)S(1)} %bitcast.170), channel_id=1, replica_groups=mesh['dp'=8,'ctx'=16] {'ctx'}, dimensions={0} | all-to-all | bytes 2097152 | tf_op jit(solution)/shard_map/all_to_all | solution.py:144
  380.5 8.1 multiply_bitcast_fusion
  388.6 17.7 %copy.157 = f32[2048,2048]{1,0:T(8,128)} copy(f32[2048,2048]{0,1:T(8,128)} %multiply_bitcast_fusion) | data formatting | bytes 33554432
  413.8 14.2 %all-to-all-done.4 = bf16[16,256,128]{2,1,0:T(8,128)(2,1)S(1)} async-done(((bf16[16,256,128]{2,1,0:T(8,128)(2,1)}), bf16[16,256,128]{2,1,0:T(8,128)(2,1)S(1)}, u32[]{:S(2)}, u32[]{:S(2)}) %all-to-all-start.4) | async-done | bytes 1048608 | tf_op jit(solution)/shard_map/all_to_all | solution.py:134
  436.8 13.8 %all-to-all-done.5 = bf16[16,256,128]{2,1,0:T(8,128)(2,1)} async-done(((bf16[16,256,128]{2,1,0:T(8,128)(2,1)}), bf16[16,256,128]{2,1,0:T(8,128)(2,1)}, u32[]{:S(2)}, u32[]{:S(2)}) %all-to-all-start.5) | async-done | bytes 1048608 | tf_op jit(solution)/shard_map/all_to_all | solution.py:141
  454.9 618.9 %reduce-scatter.4.cloned.1.call-done = f32[16,2048]{1,0:T(8,128)} async-done(((f32[2048,2048]{1,0:T(8,128)}), f32[16,2048]{1,0:T(8,128)}) %reduce-scatter.4.cloned.1.call-update) | async-done | bytes 131088
  (228 shorter events, 236.2 us)
Async XLA Ops:
  7.2 373.4 %copy-start = (bf16[1,256,2048]{2,1,0:T(8,128)(2,1)S(1)}, bf16[1,256,2048]{2,1,0:T(8,128)(2,1)}, u32[]{:S(2)}) copy-start(bf16[1,256,2048]{2,1,0:T(8,128)(2,1)} %param.13) | copy-start | bytes 3145732
  7.2 9.6 copy-start.2
  9.6 22.9 %all-to-all-start.1 = ((bf16[256,16,128]{0,2,1:T(8,128)(2,1)}), bf16[256,16,128]{0,2,1:T(8,128)(2,1)S(1)}, u32[]{:S(2)}, u32[]{:S(2)}) async-start(bf16[256,16,128]{0,2,1:T(8,128)(2,1)} %bitcast.36), calls=%async_computation.1 | async-start | bytes 2097152 | tf_op jit(solution)/shard_map/all_to_all | solution.py:121
  32.5 20.1 %all-to-all-start.3 = ((bf16[256,16,128]{0,2,1:T(8,128)(2,1)}), bf16[256,16,128]{0,2,1:T(8,128)(2,1)S(1)}, u32[]{:S(2)}, u32[]{:S(2)}) async-start(bf16[256,16,128]{0,2,1:T(8,128)(2,1)} %bitcast.175), calls=%async_computation.3 | async-start | bytes 2097152 | tf_op jit(solution)/shard_map/all_to_all | solution.py:122
  52.6 20.8 %all-to-all-start.2 = ((bf16[256,16,128]{0,2,1:T(8,128)(2,1)}), bf16[256,16,128]{0,2,1:T(8,128)(2,1)}, u32[]{:S(2)}, u32[]{:S(2)}) async-start(bf16[256,16,128]{0,2,1:T(8,128)(2,1)} %bitcast.174), calls=%async_computation.2 | async-start | bytes 2097152 | tf_op jit(solution)/shard_map/all_to_all | solution.py:123
  59.0 19.4 %copy-start.3 = (s32[1,32,3]{1,0,2:T(1,128)S(1)}, s32[1,32,3]{1,0,2:T(1,128)}, u32[]{:S(2)}) copy-start(s32[1,32,3]{1,0,2:T(1,128)} %param.15) | copy-start | bytes 1156
  59.0 19.5 %copy-start.4 = (s32[1,2]{1,0:T(1,128)S(1)}, s32[1,2]{1,0:T(1,128)}, u32[]{:S(2)}) copy-start(s32[1,2]{1,0:T(1,128)} %param.14) | copy-start | bytes 28
  73.4 20.8 %all-to-all-start = ((bf16[256,16,128]{2,0,1:T(8,128)(2,1)}), bf16[256,16,128]{2,0,1:T(8,128)(2,1)}, u32[]{:S(2)}, u32[]{:S(2)}) async-start(bf16[256,16,128]{2,0,1:T(8,128)(2,1)} %copy.123), calls=%async_computation | async-start | bytes 2097152 | tf_op jit(solution)/shard_map/all_to_all | solution.py:120
  78.4 995.5 %reduce-scatter.4.cloned.1.call-start = ((), (), s32[]{:S(2)}) async-start(), calls=%async_computation.8 | async-start | bytes 16908288
  107.5 2.6 copy-start.1
  140.3 2.6 copy-start.1
  173.0 2.6 copy-start.1
  205.6 2.6 copy-start.1
  238.4 2.6 copy-start.1
  271.2 2.6 copy-start.1
  303.9 2.6 copy-start.1
  336.7 2.6 copy-start.1
  406.3 21.7 %all-to-all-start.4 = ((bf16[16,256,128]{2,1,0:T(8,128)(2,1)}), bf16[16,256,128]{2,1,0:T(8,128)(2,1)S(1)}, u32[]{:S(2)}, u32[]{:S(2)}) async-start(bf16[16,256,128]{2,1,0:T(8,128)(2,1)} %bitcast.180), calls=%async_computation.4 | async-start | bytes 2097152 | tf_op jit(solution)/shard_map/all_to_all | solution.py:134
  428.0 22.6 %all-to-all-start.5 = ((bf16[16,256,128]{2,1,0:T(8,128)(2,1)}), bf16[16,256,128]{2,1,0:T(8,128)(2,1)}, u32[]{:S(2)}, u32[]{:S(2)}) async-start(bf16[16,256,128]{2,1,0:T(8,128)(2,1)} %bitcast.48), calls=%async_computation.5 | async-start | bytes 2097152 | tf_op jit(solution)/shard_map/all_to_all | solution.py:141
Sparse Core Ops, SparseCore 0:
  406.4 667.3 reduce-scatter.3
where the time goes:
time: 1090 us; the launch traced here: 1080 us
  waiting for transfers between devices  699 us (64%)
  local copies, waits for them, and re-layouts  126 us (12%)
  other arithmetic  108 us (10%)
  matrix products  78.3 us (7%)
  starting transfers between devices  31.4 us (3%)
  blocking collectives  18.9 us (2%)
  between operations  14.2 us (1%)
    unnamed x2, waiting for transfers between devices  619 us
    scatter-add x8, other arithmetic, advance(): key_acc.at[picks].add(key_part)  49.2 us
    scatter-add x8, other arithmetic, advance(): value_acc.at[picks].add(value_part)  49.2 us
    unnamed x17, local copies, waits for them, and re-layouts  30.2 us
    dot_general x8, matrix products, group_grads(): jnp.einsum('ghijk,gihe->gjkhe', dscore, query_tile, preferred_element_typ...  24.8 us
  transfers between devices with their start and end apart: 7, of which 7 were waited for; matrix products, arithmetic and copies ran while one was open for 2% of the time, Pallas kernels for 0%

commit v1 on v0

v1 whole, which is shorter than its diff:
```python
import functools
import math

import jax
import jax.numpy as jnp
from jax import lax
from jax.experimental import pallas as pl
from jax.experimental.pallas import tpu as pltpu
from jax.sharding import Mesh, PartitionSpec as P

D = 128
BLOCK = 128
F32 = jnp.float32
BF16 = jnp.bfloat16
LOG2E = 1.4426950408889634
DP = ("y", "zh")
CTX = ("x", "zl", "core")
NEG = float("-inf")


def pack_kernel(groups, *refs):
    count = sum(groups)
    ins, outs = refs[:count], refs[count:]
    first = 0
    for out, size in zip(outs, groups):
        rows = ins[first].shape[1]
        for n in range(size):
            for h in range(out.shape[0]):
                out[h, n * rows : (n + 1) * rows, :] = ins[first + n][0, :, h * D : (h + 1) * D]
        first += size


def pack(*groups):
    flat = [a for group in groups for a in group]
    rows, cols = flat[0].shape[1:]
    heads = cols // D
    return pl.pallas_call(
        functools.partial(pack_kernel, tuple(len(group) for group in groups)),
        out_shape=[
            jax.ShapeDtypeStruct((heads, len(group) * rows, D), BF16) for group in groups
        ],
        in_specs=[pl.BlockSpec(memory_space=pltpu.VMEM)] * len(flat),
        out_specs=[pl.BlockSpec(memory_space=pltpu.VMEM)] * len(groups),
        compiler_params=pltpu.CompilerParams(vmem_limit_bytes=24 * 1024 * 1024),
        name="pack",
        cost_estimate=pl.CostEstimate(
            flops=0, bytes_accessed=4 * rows * cols * len(flat), transcendentals=0
        ),
    )(*flat)


def unpack_kernel(count, src, *outs):
    rows = outs[0].shape[1]
    for n, out in enumerate(outs):
        for h in range(src.shape[0]):
            out[0, :, h * D : (h + 1) * D] = src[h, n * rows : (n + 1) * rows, :]


def unpack(array, count):
    heads, rows = array.shape[0], array.shape[1] // count
    return pl.pallas_call(
        functools.partial(unpack_kernel, count),
        out_shape=[jax.ShapeDtypeStruct((1, rows, heads * D), BF16)] * count,
        in_specs=[pl.BlockSpec(memory_space=pltpu.VMEM)],
        out_specs=[pl.BlockSpec(memory_space=pltpu.VMEM)] * count,
        compiler_params=pltpu.CompilerParams(vmem_limit_bytes=24 * 1024 * 1024),
        name="unpack",
        cost_estimate=pl.CostEstimate(
            flops=0, bytes_accessed=4 * rows * heads * D * count, transcendentals=0
        ),
    )(array)


def table_row(glob_ref, rand_ref, b, nb):
    left, right = b - 1, b + 1
    g0, g1 = glob_ref[0, 0], glob_ref[0, 1]
    idx = [
        jnp.maximum(left, 0),
        b,
        jnp.minimum(right, nb - 1),
        g0,
        g1,
        rand_ref[0, b, 0],
        rand_ref[0, b, 1],
        rand_ref[0, b, 2],
    ]

    def bias(c):
        return jnp.where(c, 0.0, NEG).astype(F32)

    biases = [
        bias(left >= 0),
        None,
        bias(right < nb),
        bias(jnp.abs(g0 - b) > 1),
        bias(jnp.abs(g1 - b) > 1),
        None,
        None,
        None,
    ]
    return idx, biases


def nt(a, b):
    return lax.dot_general(a, b, (((1,), (1,)), ((), ())), preferred_element_type=F32)


def probs_kernel(nb, scale, glob_ref, rand_ref, q_ref, k_ref, g_ref, p_ref, dv_ref, acc):
    step = pl.program_id(0)
    per = q_ref.shape[1]

    @pl.when(step == 0)
    def _():
        acc[...] = jnp.zeros_like(acc)

    for u in range(per):
        b = step * per + u
        idx, biases = table_row(glob_ref, rand_ref, b, nb)
        keys = jnp.concatenate([k_ref[i // 2, i % 2] for i in idx], axis=0)
        s = nt(q_ref[0, u], keys)
        tiles = [s[:, j * D : (j + 1) * D] for j in range(8)]
        tiles = [t if c is None else t + c for t, c in zip(tiles, biases)]
        top = functools.reduce(jnp.maximum, tiles)
        top = jnp.max(top, axis=1, keepdims=True)
        c2 = scale * LOG2E
        e = [jnp.exp2((t - top) * c2) for t in tiles]
        total = jnp.sum(functools.reduce(jnp.add, e), axis=1, keepdims=True)
        inv = 1.0 / total
        p = jnp.concatenate([(t * inv).astype(BF16) for t in e], axis=1)
        p_ref[u] = p
        part = jnp.dot(g_ref[0, u].T, p, preferred_element_type=F32)
        for j, i in enumerate(idx):
            acc[i] += part[:, j * D : (j + 1) * D]

    @pl.when(step == pl.num_programs(0) - 1)
    def _():
        def body(i, carry):
            dv_ref[i] = acc[i].T.astype(BF16)
            return carry

        lax.fori_loop(0, nb, body, 0)


def probs_call(glob, rand, qkg, nb, scale):
    half = nb // 2
    return pl.pallas_call(
        functools.partial(probs_kernel, nb, scale),
        grid=(half,),
        out_shape=[
            jax.ShapeDtypeStruct((nb, BLOCK, 8 * BLOCK), BF16),
            jax.ShapeDtypeStruct((nb, BLOCK, D), BF16),
        ],
        in_specs=[
            pl.BlockSpec(memory_space=pltpu.SMEM),
            pl.BlockSpec(memory_space=pltpu.SMEM),
            pl.BlockSpec((1, 2, BLOCK, D), lambda i: (i, 0, 0, 0)),
            pl.BlockSpec((half, 2, BLOCK, D), lambda i: (0, 1, 0, 0)),
            pl.BlockSpec((1, 2, BLOCK, D), lambda i: (i, 2, 0, 0)),
        ],
        out_specs=[
            pl.BlockSpec((2, BLOCK, 8 * BLOCK), lambda i: (i, 0, 0)),
            pl.BlockSpec((nb, BLOCK, D), lambda i: (0, 0, 0)),
        ],
        scratch_shapes=[pltpu.VMEM((nb, D, BLOCK), F32)],
        compiler_params=pltpu.CompilerParams(
            dimension_semantics=("arbitrary",), vmem_limit_bytes=32 * 1024 * 1024
        ),
        name="probs",
        cost_estimate=pl.CostEstimate(
            flops=4 * nb * 8 * BLOCK * BLOCK * D,
            bytes_accessed=12 * 1024 * 1024,
            transcendentals=nb * 8 * BLOCK * BLOCK,
        ),
    )(glob, rand, qkg, qkg, qkg)


def grads_kernel(nb, scale, glob_ref, rand_ref, q_ref, k_ref, g_ref, v_ref, p_ref, out_ref, acc):
    step = pl.program_id(0)
    per = q_ref.shape[1]

    @pl.when(step == 0)
    def _():
        acc[...] = jnp.zeros_like(acc)

    for u in range(per):
        b = step * per + u
        idx, _ = table_row(glob_ref, rand_ref, b, nb)
        vals = jnp.concatenate([v_ref[i // 2, i % 2] for i in idx], axis=0)
        keys = jnp.concatenate([k_ref[i // 2, i % 2] for i in idx], axis=0)
        dp = nt(g_ref[0, u], vals)
        p = p_ref[u]
        ps = [p[:, j * D : (j + 1) * D].astype(F32) for j in range(8)]
        ts = [ps[j] * dp[:, j * D : (j + 1) * D] for j in range(8)]
        delta = jnp.sum(functools.reduce(jnp.add, ts), axis=1, keepdims=True)
        ds = jnp.concatenate(
            [((t - x * delta) * scale).astype(BF16) for t, x in zip(ts, ps)], axis=1
        )
        dq = jnp.dot(ds, keys, preferred_element_type=F32)
        out_ref[step, u] = dq.astype(BF16)
        part = jnp.dot(q_ref[0, u].T, ds, preferred_element_type=F32)
        for j, i in enumerate(idx):
            acc[i] += part[:, j * D : (j + 1) * D]

    @pl.when(step == pl.num_programs(0) - 1)
    def _():
        def body(i, carry):
            out_ref[i // 2, 2 + i % 2] = acc[i].T.astype(BF16)
            return carry

        lax.fori_loop(0, nb, body, 0)


def grads_call(glob, rand, qkg, v, p, nb, scale):
    half = nb // 2
    return pl.pallas_call(
        functools.partial(grads_kernel, nb, scale),
        grid=(half,),
        out_shape=jax.ShapeDtypeStruct((half, 4, BLOCK, D), BF16),
        in_specs=[
            pl.BlockSpec(memory_space=pltpu.SMEM),
            pl.BlockSpec(memory_space=pltpu.SMEM),
            pl.BlockSpec((1, 2, BLOCK, D), lambda i: (i, 0, 0, 0)),
            pl.BlockSpec((half, 2, BLOCK, D), lambda i: (0, 1, 0, 0)),
            pl.BlockSpec((1, 2, BLOCK, D), lambda i: (i, 2, 0, 0)),
            pl.BlockSpec((half, 2, BLOCK, D), lambda i: (0, 0, 0, 0)),
            pl.BlockSpec((2, BLOCK, 8 * BLOCK), lambda i: (i, 0, 0)),
        ],
        out_specs=pl.BlockSpec((half, 4, BLOCK, D), lambda i: (0, 0, 0, 0)),
        scratch_shapes=[pltpu.VMEM((nb, D, BLOCK), F32)],
        compiler_params=pltpu.CompilerParams(
            dimension_semantics=("arbitrary",), vmem_limit_bytes=32 * 1024 * 1024
        ),
        name="grads",
        cost_estimate=pl.CostEstimate(
            flops=6 * nb * 8 * BLOCK * BLOCK * D,
            bytes_accessed=14 * 1024 * 1024,
            transcendentals=0,
        ),
    )(glob, rand, qkg, qkg, qkg, v, p)


def swap(array, axes):
    return lax.all_to_all(array, axes, split_axis=0, concat_axis=0, tiled=True)


def per_device(queries, keys, values, out_grad, layer_input, global_blocks, random_blocks):
    x = layer_input[0]
    local, features = x.shape
    n_ctx, n_dp = lax.axis_size(CTX), lax.axis_size(DP)
    nx, nz = lax.axis_size("x"), lax.axis_size(("zl", "core"))
    ny, nr = lax.axis_size("y"), lax.axis_size(("zh", "x"))
    doc = local * n_ctx
    nb = doc // BLOCK
    scale = 1.0 / math.sqrt(D)

    x_all = lax.all_gather(x, ("zl", "core"), axis=0, tiled=True)
    qkg, v_in = pack((queries, keys, out_grad), (values,))
    qkg = swap(qkg, CTX)
    qkg, v_in = lax.optimization_barrier((qkg, v_in))
    v_in = swap(v_in, CTX).reshape(n_ctx, 2, BLOCK, D)
    qkg = qkg.reshape(n_ctx, 6, BLOCK, D)
    probs, dv = probs_call(global_blocks, random_blocks, qkg, nb, scale)
    v_in, dv = lax.optimization_barrier((v_in, dv))
    dv_mid = swap(dv.reshape(nx, doc // nx, D), "x")
    qk_out = grads_call(global_blocks, random_blocks, qkg, v_in, probs, nb, scale)
    dv_mid, qk_out = lax.optimization_barrier((dv_mid, qk_out))
    qk_back = swap(qk_out.reshape(n_ctx, 2 * local, D), CTX)

    dv_cols = jnp.transpose(dv_mid, (1, 0, 2)).reshape(doc // nx, nx * D)
    w_part = lax.dot_general(
        x_all, dv_cols, (((0,), (0,)), ((), ())), preferred_element_type=F32
    ).astype(BF16)
    w_y = lax.psum_scatter(w_part, "y", scatter_dimension=0, tiled=True)
    last = ("zh", "x", "zl", "core")
    rows = features // (n_dp * n_ctx)
    w_all = swap(w_y.reshape(nr * nz, rows, nx * D), last)
    w_sum = jnp.sum(w_all.reshape(nr, nz, rows, nx, D).astype(F32), axis=0)
    w_out = jnp.transpose(w_sum, (1, 2, 0, 3)).reshape(rows, nx * nz * D)
    w_out = w_out * (1.0 / math.sqrt(doc * n_dp))

    dv_send = jnp.transpose(dv_mid.reshape(nx, nz, local, D), (1, 0, 2, 3))
    dv_back = swap(dv_send, ("zl", "core"))
    dv_out = jnp.transpose(dv_back, (2, 1, 0, 3)).reshape(local, n_ctx * D)
    dq, dk = unpack(qk_back, 2)
    return (dq, dk, dv_out[None], w_out)


def solution(mesh):
    fine = Mesh(mesh.devices.reshape(4, 2, 4, 2, 2), DP + CTX)
    tokens = P(DP, CTX, None)
    return jax.shard_map(
        per_device,
        mesh=fine,
        in_specs=(tokens,) * 5 + (P(DP, None), P(DP, None, None)),
        out_specs=(tokens, tokens, tokens, P(DP + CTX, None)),
        check_vma=False,
    )
```

time: 1090 us -> 217 us (0.20)
  waiting for transfers between devices: 699 us -> 32.2 us
  other arithmetic: 108 us -> 0.25 us
  local copies, waits for them, and re-layouts: 126 us -> 25 us
  matrix products: 78.3 us -> 6.15 us
  blocking collectives: 18.9 us -> 67.2 us
  Pallas kernels: 0 us -> 47.6 us
    unnamed x2, waiting for transfers between devices: 619 us -> 0.7 us
    scatter-add x16 -> x0, other arithmetic: 98.5 us -> none  [the longest x8 49.2 us: advance(): key_acc.at[picks].add(key_part)]
    dot_general x49 -> x1, matrix products: 78.3 us -> 6.15 us  [per_device(): lax.dot_general(x_all, dv_cols, (((0,), (0,)), ((), ())), preferred_eleme...]
    all_to_all x6 -> x4, waiting for transfers between devices: 79.6 us -> 22.8 us  [swap(): return lax.all_to_all(array, axes, split_axis=0, concat_axis=0, tiled=True)]
    all_to_all x1 -> x2, blocking collectives: 18.9 us -> 67.2 us  [swap(): return lax.all_to_all(array, axes, split_axis=0, concat_axis=0, tiled=True)]
    pallas_call x0 -> x4, Pallas kernels: none -> 47.6 us  [the longest x1 23.2 us: probs_call(): pl.pallas_call(functools.partial(probs_kernel, nb, scale), grid=(half,),...]
    gather x16 -> x0, local copies, waits for them, and re-layouts: 31.6 us -> none  [the longest x8 15.8 us: advance(): key_tile = key4[picks]]
    transpose x16 -> x0, local copies, waits for them, and re-layouts: 30.7 us -> none  [the longest x8 15.4 us: group_grads(): jnp.einsum('ghijk,gihe->gjkhe', probs_low, grad_tile, preferred_element_t...]
  transfers between devices with their start and end apart: 7 -> 6, of which waited for: 7 -> 3; matrix products, arithmetic and copies ran while one was open for 2% -> 4% of each run, Pallas kernels for 0% -> 22%
where the time goes in v1:
time: 217 us; the launch traced here: 216 us
  blocking collectives  67.2 us (31%)
  Pallas kernels  47.6 us (22%)
  waiting for transfers between devices  32.2 us (15%)
  local copies, waits for them, and re-layouts  25 us (12%)
  starting transfers between devices  23.6 us (11%)
  between operations  14.2 us (7%)
  matrix products  6.15 us (3%)
    all_to_all x2, blocking collectives, swap(): return lax.all_to_all(array, axes, split_axis=0, concat_axis=0, tiled=True)  67.2 us
    all_to_all x4, starting transfers between devices, swap(): return lax.all_to_all(array, axes, split_axis=0, concat_axis=0, tiled=True)  23.5 us
    pallas_call x1, Pallas kernels, probs_call(): pl.pallas_call(functools.partial(probs_kernel, nb, scale), grid=(half,),...  23.2 us
    all_to_all x4, waiting for transfers between devices, swap(): return lax.all_to_all(array, axes, split_axis=0, concat_axis=0, tiled=True)  22.8 us
    pallas_call x1, Pallas kernels, grads_call(): pl.pallas_call(functools.partial(grads_kernel, nb, scale), grid=(half,),...  21.8 us
    unnamed x24, local copies, waits for them, and re-layouts  16.2 us
    reduce_scatter x1, waiting for transfers between devices, per_device(): w_y = lax.psum_scatter(w_part, 'y', scatter_dimension=0, tiled=True)  8.65 us
    dot_general x1, matrix products, per_device(): lax.dot_general(x_all, dv_cols, (((0,), (0,)), ((), ())), preferred_eleme...  6.15 us
  transfers between devices with their start and end apart: 6, of which 3 were waited for; matrix products, arithmetic and copies ran while one was open for 4% of the time, Pallas kernels for 22%

profile of v1, /device:TPU:1, one launch (start us, length us, event | category | flops | bytes accessed | tf_op | source)
XLA Modules:
  0.0 216.2 jit_solution(17855286509015290976)
XLA Ops:
  9.1 1.2 copy-done.6
  10.4 1.2 copy-done.7
  11.6 1.2 copy-done.8
  13.6 50.3 %all_to_all.30 = bf16[16,768,128]{2,1,0:T(8,128)(2,1)S(1)} all-to-all(bf16[16,768,128]{2,1,0:T(8,128)(2,1)S(1)} %get-tuple-element.16), channel_id=1, replica_groups=mesh['y'=4,'zh'=2,'x'=4,'zl'=2,'core'=2] {'x','zl','core'}, dimensions={0} | all-to-all | bytes 6291456 | tf_op jit(solution)/shard_map/all_to_all | solution.py:243
  63.8 5.8 %all-to-all-start.1 = ((bf16[16,256,128]{2,1,0:T(8,128)(2,1)}), bf16[16,256,128]{2,1,0:T(8,128)(2,1)}, u32[]{:S(2)}, u32[]{:S(2)}) async-start(bf16[16,256,128]{2,1,0:T(8,128)(2,1)} %copy-done.3), calls=%async_computation.1 | async-start | bytes 2097152 | tf_op jit(solution)/shard_map/all_to_all | solution.py:243
  69.7 23.2 %probs.1 = (bf16[32,128,1024]{2,1,0:T(8,128)(2,1)S(1)}, bf16[32,128,128]{2,1,0:T(8,128)(2,1)S(1)}) custom-call(s32[1,2]{1,0:T(1,128)S(1)} %copy-done.9, s32[1,32,3]{2,1,0:T(8,128)S(1)} %copy.24.rand_ref, bf16[16,6,128,128]{3,2,1,0:T(8,128)(2,1)S(1)} %bitcast.30, bf16[16,6,128,128]{3,2,1,0:T(8,128)(2,1)S(1)} %bitcast.31, bf16[16,6,128,128]{3,2,1,0:T(8,128)(2,1)S(1)} %bitcast.32), custom_call_target="tpu_custom_call" | custom-call | flops 2147483648 | bytes 12582912 | tf_op jit(solution)/shard_map/probs/pallas_call | solution.py:146
  92.9 3.2 %copy-done = bf16[32,128,1024]{2,1,0:T(8,128)(2,1)} copy-done((bf16[32,128,1024]{2,1,0:T(8,128)(2,1)}, bf16[32,128,1024]{2,1,0:T(8,128)(2,1)S(1)}, u32[]{:S(2)}) %copy-start) | copy-done | bytes 8388632
  97.1 2.3 %copy.25 = bf16[4,1024,128]{1,2,0:T(8,128)(2,1)} copy(bf16[4,1024,128]{2,1,0:T(8,128)(2,1)} %bitcast.37) | data formatting | bytes 2097152 | tf_op jit(solution)/shard_map/reshape | solution.py:264
  99.4 4.3 %all-to-all-start.2 = ((bf16[4,1024,128]{1,2,0:T(8,128)(2,1)}), bf16[4,1024,128]{1,2,0:T(8,128)(2,1)}, u32[]{:S(2)}, u32[]{:S(2)}) async-start(bf16[4,1024,128]{1,2,0:T(8,128)(2,1)} %copy.25), calls=%async_computation.2 | async-start | bytes 2097152 | tf_op jit(solution)/shard_map/all_to_all | solution.py:243
  103.7 3.4 %copy-done.1 = bf16[32,128,1024]{2,1,0:T(8,128)(2,1)S(1)} copy-done((bf16[32,128,1024]{2,1,0:T(8,128)(2,1)S(1)}, bf16[32,128,1024]{2,1,0:T(8,128)(2,1)}, u32[]{:S(2)}) %copy-start.1) | copy-done | bytes 8388632
  107.1 21.8 %grads.1 = bf16[16,4,128,128]{3,2,1,0:T(8,128)(2,1)S(1)} custom-call(s32[1,2]{1,0:T(1,128)S(1)} %copy-done.9, s32[1,32,3]{2,1,0:T(8,128)S(1)} %copy.24.rand_ref, bf16[16,6,128,128]{3,2,1,0:T(8,128)(2,1)S(1)} %bitcast.33, bf16[16,6,128,128]{3,2,1,0:T(8,128)(2,1)S(1)} %bitcast.34, bf16[16,6,128,128]{3,2,1,0:T(8,128)(2,1)S(1)} %bitcast.35, ...), custom_call_target="tpu_custom_call" | custom-call | flops 3221225472 | bytes 14680064 | tf_op jit(solution)/shard_map/grads/pallas_call | solution.py:215
  128.9 1.3 copy-done.2
  130.2 6.2 %fusion.5 = bf16[2048,512]{0,1:T(8,128)(2,1)} fusion(bf16[1024,512]{0,1:T(8,128)(2,1)} %bitcast.8, bf16[1,1024,2048]{2,1,0:T(8,128)(2,1)} %all-gather.3.cloned.1.call-done), kind=kOutput, calls=%fused_computation.3 | convolution fusion | flops 2148532224 | bytes 7340032 | tf_op jit(solution)/shard_map/dot_general | solution.py:270
  136.4 1.3 copy.34
  137.8 16.9 %all_to_all.31 = bf16[4,4,256,128]{2,3,1,0:T(8,128)(2,1)S(1)} all-to-all(bf16[4,4,256,128]{2,3,1,0:T(8,128)(2,1)S(1)} %bitcast.38), channel_id=1, replica_groups=mesh['y'=4,'zh'=2,'x'=4,'zl'=2,'core'=2] {'zl','core'}, dimensions={0} | all-to-all | bytes 2097152 | tf_op jit(solution)/shard_map/all_to_all | solution.py:243
  154.7 5.4 %all-to-all-start.3 = ((bf16[16,512,128]{2,1,0:T(8,128)(2,1)}), bf16[16,512,128]{2,1,0:T(8,128)(2,1)S(1)}, u32[]{:S(2)}, u32[]{:S(2)}) async-start(bf16[16,512,128]{2,1,0:T(8,128)(2,1)} %bitcast.36), calls=%async_computation.3 | async-start | bytes 4194304 | tf_op jit(solution)/shard_map/all_to_all | solution.py:243
  160.0 8.7 %reduce-scatter.2.cloned.1.call-done = bf16[512,512]{0,1:T(8,128)(2,1)} async-done(((bf16[2048,512]{0,1:T(8,128)(2,1)}), bf16[512,512]{0,1:T(8,128)(2,1)}) %reduce-scatter.2.cloned.1.call-update) | async-done | bytes 524304 | tf_op jit(solution)/shard_map/reduce_scatter | solution.py:273
  168.7 2.0 copy.29
  170.7 16.2 %all-to-all-done.3.src = bf16[16,512,128]{2,1,0:T(8,128)(2,1)S(1)} async-done(((bf16[16,512,128]{2,1,0:T(8,128)(2,1)}), bf16[16,512,128]{2,1,0:T(8,128)(2,1)S(1)}, u32[]{:S(2)}, u32[]{:S(2)}) %all-to-all-start.3) | async-done | bytes 2097184 | tf_op jit(solution)/shard_map/all_to_all | solution.py:243
  187.0 8.1 %all-to-all-start.5 = ((bf16[32,16,512]{2,1,0:T(8,128)(2,1)}), bf16[32,16,512]{2,1,0:T(8,128)(2,1)}, u32[]{:S(2)}, u32[]{:S(2)}) async-start(bf16[32,16,512]{2,1,0:T(8,128)(2,1)} %bitcast.40), calls=%async_computation.6 | async-start | bytes 1048576 | tf_op jit(solution)/shard_map/all_to_all | solution.py:243
  196.1 2.3 %copy.31 = bf16[1,256,2048]{2,1,0:T(8,128)(2,1)} copy(bf16[1,256,2048]{1,2,0:T(8,128)(2,1)} %bitcast.39) | data formatting | bytes 2097152
  198.4 1.9 unpack.1
  200.3 6.6 %all-to-all-done.5 = bf16[32,16,512]{2,1,0:T(8,128)(2,1)} async-done(((bf16[32,16,512]{2,1,0:T(8,128)(2,1)}), bf16[32,16,512]{2,1,0:T(8,128)(2,1)}, u32[]{:S(2)}, u32[]{:S(2)}) %all-to-all-start.5) | async-done | bytes 524320 | tf_op jit(solution)/shard_map/all_to_all | solution.py:243
  206.9 1.4 reshape.42
  (30 shorter events, 5.9 us)
Async XLA Ops:
  7.2 123.1 %all-gather.3.cloned.1.call-start = ((), (), s32[]{:S(2)}) async-start(), calls=%async_computation.8 | async-start | bytes 5242880 | tf_op jit(solution)/shard_map/all_gather | solution.py:256
  7.9 1.2 copy-start.5
  9.1 1.2 copy-start.6
  10.4 1.2 copy-start.7
  11.6 1.2 copy-start.8
  13.5 50.3 %copy-start.3 = (bf16[16,256,128]{2,1,0:T(8,128)(2,1)}, bf16[16,256,128]{2,1,0:T(8,128)(2,1)S(1)}, u32[]{:S(2)}) copy-start(bf16[16,256,128]{2,1,0:T(8,128)(2,1)S(1)} %get-tuple-element.18) | copy-start | bytes 3145732
  13.5 56.1 %copy-start.10 = (s32[1,32,3]{1,0,2:T(1,128)S(1)}, s32[1,32,3]{1,0,2:T(1,128)}, u32[]{:S(2)}) copy-start(s32[1,32,3]{1,0,2:T(1,128)} %param.13) | copy-start | bytes 1156
  13.6 56.1 %copy-start.9 = (s32[1,2]{1,0:T(1,128)S(1)}, s32[1,2]{1,0:T(1,128)}, u32[]{:S(2)}) copy-start(s32[1,2]{1,0:T(1,128)} %glob_ref.3) | copy-start | bytes 28
  63.8 33.3 %all-to-all-start.1 = ((bf16[16,256,128]{2,1,0:T(8,128)(2,1)}), bf16[16,256,128]{2,1,0:T(8,128)(2,1)}, u32[]{:S(2)}, u32[]{:S(2)}) async-start(bf16[16,256,128]{2,1,0:T(8,128)(2,1)} %copy-done.3), calls=%async_computation.1 | async-start | bytes 2097152 | tf_op jit(solution)/shard_map/all_to_all | solution.py:243
  92.9 3.3 %copy-start = (bf16[32,128,1024]{2,1,0:T(8,128)(2,1)}, bf16[32,128,1024]{2,1,0:T(8,128)(2,1)S(1)}, u32[]{:S(2)}) copy-start(bf16[32,128,1024]{2,1,0:T(8,128)(2,1)S(1)} %get-tuple-element.23.p_ref) | copy-start | bytes 25165828
  96.1 1.0 copy-start.4
  99.4 30.9 %all-to-all-start.2 = ((bf16[4,1024,128]{1,2,0:T(8,128)(2,1)}), bf16[4,1024,128]{1,2,0:T(8,128)(2,1)}, u32[]{:S(2)}, u32[]{:S(2)}) async-start(bf16[4,1024,128]{1,2,0:T(8,128)(2,1)} %copy.25), calls=%async_computation.2 | async-start | bytes 2097152 | tf_op jit(solution)/shard_map/all_to_all | solution.py:243
  103.6 65.1 %reduce-scatter.2.cloned.1.call-start = ((), (), s32[]{:S(2)}) async-start(), calls=%async_computation.7 | async-start | bytes 2621440 | tf_op jit(solution)/shard_map/reduce_scatter | solution.py:273
  103.7 3.4 %copy-start.1 = (bf16[32,128,1024]{2,1,0:T(8,128)(2,1)S(1)}, bf16[32,128,1024]{2,1,0:T(8,128)(2,1)}, u32[]{:S(2)}) copy-start(bf16[32,128,1024]{2,1,0:T(8,128)(2,1)} %copy-done) | copy-start | bytes 25165828
  128.9 1.3 copy-start.2
  154.7 32.3 %all-to-all-start.3 = ((bf16[16,512,128]{2,1,0:T(8,128)(2,1)}), bf16[16,512,128]{2,1,0:T(8,128)(2,1)S(1)}, u32[]{:S(2)}, u32[]{:S(2)}) async-start(bf16[16,512,128]{2,1,0:T(8,128)(2,1)} %bitcast.36), calls=%async_computation.3 | async-start | bytes 4194304 | tf_op jit(solution)/shard_map/all_to_all | solution.py:243
  187.0 19.9 %all-to-all-start.5 = ((bf16[32,16,512]{2,1,0:T(8,128)(2,1)}), bf16[32,16,512]{2,1,0:T(8,128)(2,1)}, u32[]{:S(2)}, u32[]{:S(2)}) async-start(bf16[32,16,512]{2,1,0:T(8,128)(2,1)} %bitcast.40), calls=%async_computation.6 | async-start | bytes 1048576 | tf_op jit(solution)/shard_map/all_to_all | solution.py:243
Sparse Core Ops, SparseCore 0:
  9.7 92.7 all-gather.2
  136.5 32.1 reduce-scatter.1

commit v2 on v1

v2 whole, which is shorter than its diff:
```python
import functools
import math

import jax
import jax.numpy as jnp
from jax import lax
from jax.experimental import pallas as pl
from jax.experimental.pallas import tpu as pltpu
from jax.sharding import Mesh, PartitionSpec as P

D = 128
BLOCK = 128
F32 = jnp.float32
BF16 = jnp.bfloat16
LOG2E = 1.4426950408889634
DP = ("y", "zh")
CTX = ("x", "zl", "core")
NEG = float("-inf")


def hbm(array):
    return pltpu.with_memory_space_constraint(array, pltpu.HBM)


def pack_kernel(groups, *refs):
    count = sum(groups)
    ins, outs = refs[:count], refs[count : count + len(groups)]
    bufs, sems = refs[count + len(groups)], refs[count + len(groups) + 1]
    copies = [pltpu.make_async_copy(src.at[0], bufs.at[n], sems.at[n]) for n, src in enumerate(ins)]
    for c in copies:
        c.start()
    first = 0
    for out, size in zip(outs, groups):
        rows = bufs.shape[1]
        for n in range(size):
            copies[first + n].wait()
            for h in range(out.shape[0]):
                out[h, n * rows : (n + 1) * rows, :] = bufs[first + n, :, h * D : (h + 1) * D]
        first += size


def pack(*groups):
    flat = [a for group in groups for a in group]
    rows, cols = flat[0].shape[1:]
    heads = cols // D
    return pl.pallas_call(
        functools.partial(pack_kernel, tuple(len(group) for group in groups)),
        out_shape=[pltpu.HBM((heads, len(group) * rows, D), BF16) for group in groups],
        in_specs=[pl.BlockSpec(memory_space=pl.ANY)] * len(flat),
        out_specs=[pl.BlockSpec(memory_space=pltpu.VMEM)] * len(groups),
        scratch_shapes=[
            pltpu.VMEM((len(flat), rows, cols), BF16),
            pltpu.SemaphoreType.DMA((len(flat),)),
        ],
        compiler_params=pltpu.CompilerParams(vmem_limit_bytes=24 * 1024 * 1024),
        name="pack",
        cost_estimate=pl.CostEstimate(
            flops=0, bytes_accessed=4 * rows * cols * len(flat), transcendentals=0
        ),
    )(*[hbm(a) for a in flat])


def unpack_kernel(count, src, *outs):
    rows = outs[0].shape[1]
    for n, out in enumerate(outs):
        for h in range(src.shape[0]):
            out[0, :, h * D : (h + 1) * D] = src[h, n * rows : (n + 1) * rows, :]


def unpack(array, count):
    heads, rows = array.shape[0], array.shape[1] // count
    return pl.pallas_call(
        functools.partial(unpack_kernel, count),
        out_shape=[jax.ShapeDtypeStruct((1, rows, heads * D), BF16)] * count,
        in_specs=[pl.BlockSpec(memory_space=pltpu.VMEM)],
        out_specs=[pl.BlockSpec(memory_space=pltpu.VMEM)] * count,
        compiler_params=pltpu.CompilerParams(vmem_limit_bytes=24 * 1024 * 1024),
        name="unpack",
        cost_estimate=pl.CostEstimate(
            flops=0, bytes_accessed=4 * rows * heads * D * count, transcendentals=0
        ),
    )(array)


def table_row(glob_ref, rand_ref, b, nb):
    left, right = b - 1, b + 1
    g0, g1 = glob_ref[0, 0], glob_ref[0, 1]
    idx = [
        jnp.maximum(left, 0),
        b,
        jnp.minimum(right, nb - 1),
        g0,
        g1,
        rand_ref[0, b, 0],
        rand_ref[0, b, 1],
        rand_ref[0, b, 2],
    ]

    def bias(c):
        return jnp.where(c, 0.0, NEG).astype(F32)

    biases = [
        bias(left >= 0),
        None,
        bias(right < nb),
        bias(jnp.abs(g0 - b) > 1),
        bias(jnp.abs(g1 - b) > 1),
        None,
        None,
        None,
    ]
    return idx, biases


def nt(a, b):
    return lax.dot_general(a, b, (((1,), (1,)), ((), ())), preferred_element_type=F32)


def tn(a, b):
    return lax.dot_general(a, b, (((0,), (0,)), ((), ())), preferred_element_type=F32)


def diag(a, b):
    zero = jnp.zeros_like(a)
    return jnp.concatenate(
        [jnp.concatenate([a, zero], axis=1), jnp.concatenate([zero, b], axis=1)], axis=0
    )


def pick(ref, idx):
    return jnp.concatenate([ref[i // 2, i % 2] for i in idx], axis=0)


def tile(array, j, half):
    return array[j * D : (j + 1) * D, half * D : (half + 1) * D]


def add_tiles(acc, idx_pair, part):
    for j in range(8):
        for half, idx in enumerate(idx_pair):
            acc[idx[j]] += tile(part, j, half)


def probs_kernel(
    nb, nx, scale, glob_ref, rand_ref, me_ref, q_ref, k_ref, g_ref, p_ref, dv_ref, *rest
):
    parts, acc = rest[:-1], rest[-1]
    step = pl.program_id(0)
    pairs = q_ref.shape[0]

    @pl.when(step == 0)
    def _():
        acc[...] = jnp.zeros_like(acc)

    for u in range(pairs):
        b = (step * pairs + u) * 2
        rows = [table_row(glob_ref, rand_ref, b + half, nb) for half in range(2)]
        idx_pair = [row[0] for row in rows]
        keys = jnp.concatenate([pick(k_ref, idx) for idx in idx_pair], axis=1)
        s = nt(keys, diag(q_ref[u, 0], q_ref[u, 1]))
        ps = []
        for half, (_, biases) in enumerate(rows):
            tiles = [tile(s, j, half) for j in range(8)]
            tiles = [t if c is None else t + c for t, c in zip(tiles, biases)]
            top = jnp.max(functools.reduce(jnp.maximum, tiles), axis=0, keepdims=True)
            e = [jnp.exp2((t - top) * (scale * LOG2E)) for t in tiles]
            inv = 1.0 / jnp.sum(functools.reduce(jnp.add, e), axis=0, keepdims=True)
            ps.append(jnp.concatenate([(t * inv).astype(BF16) for t in e], axis=0))
        p = jnp.concatenate(ps, axis=1)
        p_ref[u] = p
        part = jnp.dot(p, diag(g_ref[u, 0], g_ref[u, 1]), preferred_element_type=F32)
        add_tiles(acc, idx_pair, part)

    @pl.when(step == pl.num_programs(0) - 1)
    def _():
        dv_ref[...] = acc[...].astype(BF16).reshape(dv_ref.shape)
        size = parts[0].shape[0]
        for n, part in enumerate(parts):
            part[...] = dv_ref[pl.ds(lax.rem(me_ref[0] + n, nx) * size, size)]


def probs_call(glob, rand, me, qkg, nb, nx, scale):
    half, pairs = nb // 2, 4
    return pl.pallas_call(
        functools.partial(probs_kernel, nb, nx, scale),
        grid=(half // pairs,),
        out_shape=[
            pltpu.HBM((half, 8 * BLOCK, 2 * BLOCK), BF16),
            pltpu.HBM((half, 2, BLOCK, D), BF16),
        ]
        + [pltpu.HBM((half // nx, 2, BLOCK, D), BF16)] * nx,
        in_specs=[pl.BlockSpec(memory_space=pltpu.SMEM)] * 3
        + [
            pl.BlockSpec((pairs, 2, BLOCK, D), lambda i: (i, 0, 0, 0)),
            pl.BlockSpec((half, 2, BLOCK, D), lambda i: (0, 1, 0, 0)),
            pl.BlockSpec((pairs, 2, BLOCK, D), lambda i: (i, 2, 0, 0)),
        ],
        out_specs=[
            pl.BlockSpec((pairs, 8 * BLOCK, 2 * BLOCK), lambda i: (i, 0, 0)),
            pl.BlockSpec((half, 2, BLOCK, D), lambda i: (0, 0, 0, 0)),
        ]
        + [pl.BlockSpec((half // nx, 2, BLOCK, D), lambda i: (0, 0, 0, 0))] * nx,
        scratch_shapes=[pltpu.VMEM((nb, BLOCK, D), F32)],
        compiler_params=pltpu.CompilerParams(
            dimension_semantics=("arbitrary",), vmem_limit_bytes=32 * 1024 * 1024
        ),
        name="probs",
        cost_estimate=pl.CostEstimate(
            flops=8 * nb * 8 * BLOCK * BLOCK * D,
            bytes_accessed=14 * 1024 * 1024,
            transcendentals=nb * 8 * BLOCK * BLOCK,
        ),
    )(glob, rand, me, qkg, qkg, qkg)


def grads_kernel(
    nb, scale, glob_ref, rand_ref, q_ref, k_ref, g_ref, v_ref, p_ref, dv_ref, out_ref, acc
):
    step = pl.program_id(0)
    pairs = q_ref.shape[0]

    @pl.when(step == 0)
    def _():
        acc[...] = jnp.zeros_like(acc)

    for u in range(pairs):
        b = (step * pairs + u) * 2
        idx_pair = [table_row(glob_ref, rand_ref, b + half, nb)[0] for half in range(2)]
        vals = jnp.concatenate([pick(v_ref, idx) for idx in idx_pair], axis=1)
        dp = nt(vals, diag(g_ref[u, 0], g_ref[u, 1]))
        both = []
        for half, idx in enumerate(idx_pair):
            ps = [tile(p_ref[u], j, half).astype(F32) for j in range(8)]
            ts = [ps[j] * tile(dp, j, half) for j in range(8)]
            delta = jnp.sum(functools.reduce(jnp.add, ts), axis=0, keepdims=True)
            ds = jnp.concatenate([(t - x * delta).astype(BF16) for t, x in zip(ts, ps)], axis=0)
            both.append(ds)
            dq = tn(ds, pick(k_ref, idx)) * scale
            out_ref[step * pairs + u, half] = dq.astype(BF16)
        ds = jnp.concatenate(both, axis=1)
        part = jnp.dot(ds, diag(q_ref[u, 0], q_ref[u, 1]), preferred_element_type=F32)
        add_tiles(acc, idx_pair, part)

    @pl.when(step == pl.num_programs(0) - 1)
    def _():
        out_ref[:, 2:4] = (acc[...] * scale).astype(BF16).reshape(nb // 2, 2, BLOCK, D)
        out_ref[:, 4:6] = dv_ref[...]


def grads_call(glob, rand, qkg, v, p, dv, nb, scale):
    half, pairs = nb // 2, 4
    return pl.pallas_call(
        functools.partial(grads_kernel, nb, scale),
        grid=(half // pairs,),
        out_shape=pltpu.HBM((half, 6, BLOCK, D), BF16),
        in_specs=[pl.BlockSpec(memory_space=pltpu.SMEM)] * 2
        + [
            pl.BlockSpec((pairs, 2, BLOCK, D), lambda i: (i, 0, 0, 0)),
            pl.BlockSpec((half, 2, BLOCK, D), lambda i: (0, 1, 0, 0)),
            pl.BlockSpec((pairs, 2, BLOCK, D), lambda i: (i, 2, 0, 0)),
            pl.BlockSpec((half, 2, BLOCK, D), lambda i: (0, 0, 0, 0)),
            pl.BlockSpec((pairs, 8 * BLOCK, 2 * BLOCK), lambda i: (i, 0, 0)),
            pl.BlockSpec((half, 2, BLOCK, D), lambda i: (0, 0, 0, 0)),
        ],
        out_specs=pl.BlockSpec((half, 6, BLOCK, D), lambda i: (0, 0, 0, 0)),
        scratch_shapes=[pltpu.VMEM((nb, BLOCK, D), F32)],
        compiler_params=pltpu.CompilerParams(
            dimension_semantics=("arbitrary",), vmem_limit_bytes=32 * 1024 * 1024
        ),
        name="grads",
        cost_estimate=pl.CostEstimate(
            flops=10 * nb * 8 * BLOCK * BLOCK * D,
            bytes_accessed=14 * 1024 * 1024,
            transcendentals=0,
        ),
    )(glob, rand, qkg, qkg, qkg, v, hbm(p), hbm(dv))


def weight_kernel(count, nx, nz, ny, me_ref, *refs):
    xs, parts, refs = refs[:count], refs[count : count + nx], refs[count + nx :]
    outs, cols = refs[:ny], refs[ny]
    rows = cols.shape[0] // nz
    step = pl.program_id(0)

    @pl.when(step == 0)
    def _():
        for n, part in enumerate(parts):
            head = pl.multiple_of(lax.rem(me_ref[0] + nx - n, nx) * D, D)
            for m in range(nz):
                first = pl.multiple_of((me_ref[1] ^ m) * rows, rows)
                cols[m * rows : (m + 1) * rows, pl.ds(head, D)] = part[pl.ds(first, rows), :]

    x = jnp.concatenate([ref[0] for ref in xs], axis=0)
    w = tn(x, cols[...]).astype(BF16)
    for n, out in enumerate(outs):

        @pl.when(step == n)
        def _():
            out[...] = w


def weight_call(me, xs, parts, nz, ny):
    nx, tokens = len(parts), parts[0].shape[0]
    features = xs[0].shape[2]
    size = features // ny
    grid_spec = pltpu.PrefetchScalarGridSpec(
        num_scalar_prefetch=1,
        grid=(ny,),
        in_specs=[
            pl.BlockSpec((1, x.shape[1], size), lambda i, me: (0, 0, lax.rem(me[2] + i, ny)))
            for x in xs
        ]
        + [pl.BlockSpec(parts[0].shape, lambda i, me: (0, 0))] * nx,
        out_specs=[pl.BlockSpec((size, nx * D), lambda i, me: (0, 0))] * ny,
        scratch_shapes=[pltpu.VMEM((tokens, nx * D), BF16)],
    )
    return pl.pallas_call(
        functools.partial(weight_kernel, len(xs), nx, nz, ny),
        grid_spec=grid_spec,
        out_shape=[pltpu.HBM((size, nx * D), BF16)] * ny,
        compiler_params=pltpu.CompilerParams(
            dimension_semantics=("arbitrary",), vmem_limit_bytes=24 * 1024 * 1024
        ),
        name="weight",
        cost_estimate=pl.CostEstimate(
            flops=2 * tokens * features * nx * D,
            bytes_accessed=7 * 1024 * 1024,
            transcendentals=0,
        ),
    )(me, *[hbm(x) for x in xs], *[hbm(part) for part in parts])


def add_kernel(*refs):
    total = refs[0][...].astype(F32)
    for ref in refs[1:-1]:
        total = total + ref[...].astype(F32)
    refs[-1][...] = total.astype(BF16)


def add_call(arrays):
    shape = arrays[0].shape
    return pl.pallas_call(
        add_kernel,
        out_shape=pltpu.HBM(shape, BF16),
        in_specs=[pl.BlockSpec(memory_space=pltpu.VMEM)] * len(arrays),
        out_specs=pl.BlockSpec(memory_space=pltpu.VMEM),
        name="add",
        cost_estimate=pl.CostEstimate(
            flops=arrays[0].size * 3, bytes_accessed=arrays[0].size * 10, transcendentals=0
        ),
    )(*arrays)


def sum_kernel(nz, nx, scale, in_ref, out_ref):
    for n in range(nz):
        total = in_ref[n].astype(F32)
        for r in range(1, in_ref.shape[0] // nz):
            total = total + in_ref[r * nz + n].astype(F32)
        total = total * scale
        for h in range(nx):
            c = (h * nz + n) * D
            out_ref[:, c : c + D] = total[:, h * D : (h + 1) * D]


def sum_call(array, nz, nx, scale):
    rows = array.shape[1]
    return pl.pallas_call(
        functools.partial(sum_kernel, nz, nx, scale),
        out_shape=jax.ShapeDtypeStruct((rows, nz * nx * D), F32),
        in_specs=[pl.BlockSpec(memory_space=pltpu.VMEM)],
        out_specs=pl.BlockSpec(memory_space=pltpu.VMEM),
        name="sum",
        cost_estimate=pl.CostEstimate(
            flops=array.size, bytes_accessed=2 * array.size, transcendentals=0
        ),
    )(array)


def swap(array, axes):
    return lax.all_to_all(array, axes, split_axis=0, concat_axis=0, tiled=True)


def shift(array, axis, n, size):
    return lax.ppermute(array, axis, [(i, (i + n) % size) for i in range(size)])


def per_device(queries, keys, values, out_grad, layer_input, global_blocks, random_blocks):
    local, features = layer_input.shape[1:]
    n_ctx, n_dp = lax.axis_size(CTX), lax.axis_size(DP)
    nx, ny, nz = lax.axis_size("x"), lax.axis_size("y"), lax.axis_size(("zl", "core"))
    nr = lax.axis_size(("zh", "x"))
    doc = local * n_ctx
    nb = doc // BLOCK
    scale = 1.0 / math.sqrt(D)
    me = [lax.axis_index("x"), lax.axis_index(("zl", "core")), lax.axis_index("y")]
    me = jnp.stack(me).astype(jnp.int32)

    qkg, v_in = pack((queries, keys, out_grad), (values,))
    qkg = swap(qkg, CTX)
    qkg, v_in, x_own = lax.optimization_barrier((qkg, v_in, layer_input))
    v_in = swap(v_in, CTX).reshape(n_ctx, 2, BLOCK, D)
    qkg = qkg.reshape(n_ctx, 6, BLOCK, D)
    probs, dv, *parts = probs_call(global_blocks, random_blocks, me, qkg, nb, nx, scale)
    parts = [part.reshape(doc // nx, D) for part in parts]
    cut = local * 3 // 8
    x_core = shift(x_own, "core", 1, 2)
    x_zl = [shift(x_own[:, :cut], "zl", 1, 2)]
    v_in, x_own, x_core, x_zl[0], *parts = lax.optimization_barrier(
        (v_in, x_own, x_core, x_zl[0], *parts)
    )
    parts = parts[:1] + [shift(parts[n], "x", n, nx) for n in range(1, nx)]
    x_zl.append(shift(x_own[:, cut:], "zl", 1, 2))
    x_both = [shift(x_zl[0], "core", 1, 2)]
    qkv = grads_call(global_blocks, random_blocks, qkg, v_in, probs, dv, nb, scale)
    qkv, x_zl[1], x_both[0], *parts = lax.optimization_barrier((qkv, x_zl[1], x_both[0], *parts))
    back = swap(qkv.reshape(n_ctx, 3 * local, D), CTX)
    x_both.append(shift(x_zl[1], "core", 1, 2))
    xs = [x_own, x_core, *x_zl, *x_both]
    w_parts = weight_call(me, xs, parts, nz, ny)
    w_y = add_call([w_parts[0]] + [shift(w_parts[n], "y", n, ny) for n in range(1, ny)])

    rows = features // (n_dp * n_ctx)
    w_y, back = lax.optimization_barrier((w_y, back))
    w_all = swap(w_y.reshape(nr * nz, rows, nx * D), ("zh", "x", "zl", "core"))
    w_out = sum_call(w_all, nz, nx, 1.0 / math.sqrt(doc * n_dp))
    dq, dk, dv_out = unpack(back, 3)
    return (dq, dk, dv_out, w_out)


def solution(mesh):
    fine = Mesh(mesh.devices.reshape(4, 2, 4, 2, 2), DP + CTX)
    tokens = P(DP, CTX, None)
    return jax.shard_map(
        per_device,
        mesh=fine,
        in_specs=(tokens,) * 5 + (P(DP, None), P(DP, None, None)),
        out_specs=(tokens, tokens, tokens, P(DP + CTX, None)),
        check_vma=False,
    )
```

time: 217 us -> 173 us (0.80)
  blocking collectives: 67.2 us -> 44.9 us
  local copies, waits for them, and re-layouts: 25 us -> 4.87 us
  between operations: 14.2 us -> 0.78 us
  starting transfers between devices: 23.6 us -> 31.5 us
  waiting for transfers between devices: 32.2 us -> 38.5 us
  matrix products: 6.15 us -> 0 us
  Pallas kernels: 47.6 us -> 51.4 us
    ppermute x0 -> x11, waiting for transfers between devices: none -> 29.3 us  [shift(): return lax.ppermute(array, axis, [(i, (i + n) % size) for i in range(size)])]
    all_to_all x2 -> x1, blocking collectives: 67.2 us -> 44.9 us  [swap(): return lax.all_to_all(array, axes, split_axis=0, concat_axis=0, tiled=True)]
    ppermute x0 -> x11, starting transfers between devices: none -> 15.1 us  [shift(): return lax.ppermute(array, axis, [(i, (i + n) % size) for i in range(size)])]
    all_to_all x4 -> x3, waiting for transfers between devices: 22.8 us -> 9.27 us  [swap(): return lax.all_to_all(array, axes, split_axis=0, concat_axis=0, tiled=True)]
    unnamed x24 -> x17, local copies, waits for them, and re-layouts: 16.2 us -> 2.7 us
    reduce_scatter x1 -> x0, waiting for transfers between devices: 8.65 us -> none  [per_device(): w_y = lax.psum_scatter(w_part, 'y', scatter_dimension=0, tiled=True)]
    all_to_all x4 -> x3, starting transfers between devices: 23.5 us -> 16.4 us  [swap(): return lax.all_to_all(array, axes, split_axis=0, concat_axis=0, tiled=True)]
    dot_general x1 -> x0, matrix products: 6.15 us -> none  [per_device(): lax.dot_general(x_all, dv_cols, (((0,), (0,)), ((), ())), preferred_eleme...]
  transfers between devices with their start and end apart: 6 -> 14, of which waited for: 3 -> 5; matrix products, arithmetic and copies ran while one was open for 4% -> 1% of each run, Pallas kernels for 22% -> 26%
where the time goes in v2:
time: 173 us; the launch traced here: 172 us
  Pallas kernels  51.4 us (30%)
  blocking collectives  44.9 us (26%)
  waiting for transfers between devices  38.5 us (22%)
  starting transfers between devices  31.5 us (18%)
  local copies, waits for them, and re-layouts  4.87 us (3%)
    all_to_all x1, blocking collectives, swap(): return lax.all_to_all(array, axes, split_axis=0, concat_axis=0, tiled=True)  44.9 us
    ppermute x11, waiting for transfers between devices, shift(): return lax.ppermute(array, axis, [(i, (i + n) % size) for i in range(size)])  29.3 us
    pallas_call x1, Pallas kernels, grads_call(): pl.pallas_call(functools.partial(grads_kernel, nb, scale), grid=(half //...  17.7 us
    all_to_all x3, starting transfers between devices, swap(): return lax.all_to_all(array, axes, split_axis=0, concat_axis=0, tiled=True)  16.4 us
    ppermute x11, starting transfers between devices, shift(): return lax.ppermute(array, axis, [(i, (i + n) % size) for i in range(size)])  15.1 us
    pallas_call x1, Pallas kernels, probs_call(): pl.pallas_call(functools.partial(probs_kernel, nb, nx, scale), grid=(half...  14.8 us
    all_to_all x3, waiting for transfers between devices, swap(): return lax.all_to_all(array, axes, split_axis=0, concat_axis=0, tiled=True)  9.27 us
    pallas_call x1, Pallas kernels, weight_call(): pl.pallas_call(functools.partial(weight_kernel, len(xs), nx, nz, ny), gri...  7.6 us
  transfers between devices with their start and end apart: 14, of which 5 were waited for; matrix products, arithmetic and copies ran while one was open for 1% of the time, Pallas kernels for 26%

profile of v2, /device:TPU:1, one launch (start us, length us, event | category | flops | bytes accessed | tf_op | source)
XLA Modules:
  0.0 172.0 jit_solution(12813019317581878181)
XLA Ops:
  0.6 4.4 %pack.1 = (bf16[16,768,128]{2,1,0:T(8,128)(2,1)}, bf16[16,256,128]{2,1,0:T(8,128)(2,1)}) custom-call(bf16[1,256,2048]{2,1,0:T(8,128)(2,1)} %refs_0_.1, bf16[1,256,2048]{2,1,0:T(8,128)(2,1)} %refs_1_.1, bf16[1,256,2048]{2,1,0:T(8,128)(2,1)} %refs_2_.1, bf16[1,256,2048]{2,1,0:T(8,128)(2,1)} %refs_3_.1), custom_call_target="tpu_custom_call" | custom-call | bytes 8388608 | tf_op jit(solution)/shard_map/pack/pallas_call | solution.py:46
  5.0 44.9 %all_to_all.20 = bf16[16,768,128]{2,1,0:T(8,128)(2,1)S(1)} all-to-all(bf16[16,768,128]{2,1,0:T(8,128)(2,1)} %get-tuple-element.39), channel_id=1, replica_groups=mesh['y'=4,'zh'=2,'x'=4,'zl'=2,'core'=2] {'x','zl','core'}, dimensions={0} | all-to-all | bytes 6291456 | tf_op jit(solution)/shard_map/all_to_all | solution.py:380
  49.9 1.3 collective-permute-start
  51.3 4.3 %all-to-all-start.1 = ((bf16[16,256,128]{2,1,0:T(8,128)(2,1)}), bf16[16,256,128]{2,1,0:T(8,128)(2,1)}, u32[]{:S(2)}, u32[]{:S(2)}) async-start(bf16[16,256,128]{2,1,0:T(8,128)(2,1)} %get-tuple-element.41), calls=%async_computation.1 | async-start | bytes 2097152 | tf_op jit(solution)/shard_map/all_to_all | solution.py:380
  56.7 1.3 collective-permute-start.1
  58.0 14.8 %probs.1 = (bf16[16,1024,256]{2,1,0:T(8,128)(2,1)}, bf16[16,2,128,128]{3,2,1,0:T(8,128)(2,1)}, bf16[4,2,128,128]{3,2,1,0:T(8,128)(2,1)}, bf16[4,2,128,128]{3,2,1...) custom-call(s32[1,2]{1,0:T(1,128)S(1)} %copy-done, s32[1,32,3]{2,1,0:T(8,128)S(1)} %copy.11.rand_ref, ...), custom_call_target="tpu_custom_call" | custom-call | flops 4294967296 | bytes 14680064 | tf_op jit(solution)/shard_map/probs/pallas_call | solution.py:184
  72.8 4.6 %collective-permute-done.1.refs_2_ = bf16[1,96,2048]{2,1,0:T(8,128)(2,1)} collective-permute-done((bf16[1,96,2048]{2,1,0:T(8,128)(2,1)S(1)}, bf16[1,96,2048]{2,1,0:T(8,128)(2,1)}, u32[]{:S(2)}, u32[]{:S(2)}) %collective-permute-start.1) | collective-permute-done | bytes 393248 | tf_op jit(solution)/shard_map/ppermute | solution.py:384
  77.5 1.1 slice.7
  78.9 1.3 collective-permute-start.4
  80.2 2.6 %collective-permute-start.5 = (bf16[1024,128]{1,0:T(8,128)(2,1)}, bf16[1024,128]{1,0:T(8,128)(2,1)S(1)}, u32[]{:S(2)}, u32[]{:S(2)}) collective-permute-start(bf16[1024,128]{1,0:T(8,128)(2,1)} %bitcast.20), channel_id=1, source_target_pairs={{0,8},{4,12},{8,0},{12,4},{1,9},{5,13},{9,1},{13,5},{2,10},{6,14},... | collective-permute-start | bytes 786440 | tf_op jit(solution)/shard_map/ppermute | solution.py:384
  83.8 2.0 %collective-permute-start.3 = (bf16[1,96,2048]{2,1,0:T(8,128)(2,1)}, bf16[1,96,2048]{2,1,0:T(8,128)(2,1)S(1)}, u32[]{:S(2)}, u32[]{:S(2)}) collective-permute-start(bf16[1,96,2048]{2,1,0:T(8,128)(2,1)} %collective-permute-done.1.refs_2_), channel_id=1, source_target_pairs={{0,1},{1,0},{2,3},{3,2},{4,5},{5,4},{6,7},{7,6},{8,9},{9,8},{10,11... | collective-permute-start | bytes 1179656 | tf_op jit(solution)/shard_map/ppermute | solution.py:384
  85.8 17.7 %grads.1 = bf16[16,6,128,128]{3,2,1,0:T(8,128)(2,1)} custom-call(s32[1,2]{1,0:T(1,128)S(1)} %copy-done, s32[1,32,3]{2,1,0:T(8,128)S(1)} %copy.11.rand_ref, bf16[16,6,128,128]{3,2,1,0:T(8,128)(2,1)S(1)} %bitcast.14, bf16[16,6,128,128]{3,2,1,0:T(8,128)(2,1)S(1)} %bitcast.15, bf16[16,6,128,128]{3,2,1,0:T(8,128)(2,1)S(1)} %bitcast.16, ...), custom_call_target="tpu_custom_call" | custom-call | flops 5368709120 | bytes 14680064 | tf_op jit(solution)/shard_map/grads/pallas_call | solution.py:252
  105.3 3.6 %all-to-all-start.2 = ((bf16[16,768,128]{2,1,0:T(8,128)(2,1)}), bf16[16,768,128]{2,1,0:T(8,128)(2,1)S(1)}, u32[]{:S(2)}, u32[]{:S(2)}) async-start(bf16[16,768,128]{2,1,0:T(8,128)(2,1)} %bitcast.17), calls=%async_computation.2 | async-start | bytes 6291456 | tf_op jit(solution)/shard_map/all_to_all | solution.py:380
  109.3 2.2 %collective-permute-done.7.refs_5_ = bf16[1,160,2048]{2,1,0:T(8,128)(2,1)S(1)} collective-permute-done((bf16[1,160,2048]{2,1,0:T(8,128)(2,1)}, bf16[1,160,2048]{2,1,0:T(8,128)(2,1)S(1)}, u32[]{:S(2)}, u32[]{:S(2)}) %collective-permute-start.7) | collective-permute-done | bytes 655392 | tf_op jit(solution)/shard_map/ppermute | solution.py:384
  112.4 7.6 %weight.1 = (bf16[512,512]{1,0:T(8,128)(2,1)}, bf16[512,512]{1,0:T(8,128)(2,1)}, bf16[512,512]{1,0:T(8,128)(2,1)}, bf16[512,512]{1,0:T(8,128)(2,1)}) custom-call(s32[3]{0:T(128)S(1)} %pad_add_fusion.me_ref, bf16[1,256,2048]{2,1,0:T(8,128)(2,1)} %refs_0_.2, bf16[1,256,2048]{2,1,0:T(8,128)(2,1)} %collective-permute-done.refs_1_, ...), custom_call_target="tpu_custom_call" | custom-call | flops 2147483648 | bytes 7340032 | tf_op jit(solution)/shard_map/weight/pallas_call | solution.py:317
  120.0 1.3 collective-permute-start.8
  121.3 2.6 %collective-permute-start.9 = (bf16[512,512]{1,0:T(8,128)(2,1)}, bf16[512,512]{1,0:T(8,128)(2,1)}, u32[]{:S(2)}, u32[]{:S(2)}) collective-permute-start(bf16[512,512]{1,0:T(8,128)(2,1)} %get-tuple-element.66), channel_id=1, source_target_pairs={{0,64},{32,96},{64,0},{96,32},{1,65},{33,97},{65,1},{97,33},{2,66}... | collective-permute-start | bytes 1572872 | tf_op jit(solution)/shard_map/ppermute | solution.py:384
  125.0 10.1 %collective-permute-done.8.refs_1_ = bf16[512,512]{1,0:T(8,128)(2,1)} collective-permute-done((bf16[512,512]{1,0:T(8,128)(2,1)}, bf16[512,512]{1,0:T(8,128)(2,1)}, u32[]{:S(2)}, u32[]{:S(2)}) %collective-permute-start.8) | collective-permute-done | bytes 524320 | tf_op jit(solution)/shard_map/ppermute | solution.py:384
  135.0 12.3 %collective-permute-done.9.refs_2_ = bf16[512,512]{1,0:T(8,128)(2,1)} collective-permute-done((bf16[512,512]{1,0:T(8,128)(2,1)}, bf16[512,512]{1,0:T(8,128)(2,1)}, u32[]{:S(2)}, u32[]{:S(2)}) %collective-permute-start.9) | collective-permute-done | bytes 524320 | tf_op jit(solution)/shard_map/ppermute | solution.py:384
  147.4 2.6 %add.9 = bf16[512,512]{1,0:T(8,128)(2,1)} custom-call(bf16[512,512]{1,0:T(8,128)(2,1)} %get-tuple-element.64.refs_0_, bf16[512,512]{1,0:T(8,128)(2,1)} %collective-permute-done.8.refs_1_, bf16[512,512]{1,0:T(8,128)(2,1)} %collective-permute-done.9.refs_2_, bf16[512,512]{1,0:T(8,128)(2,1)} %collective-permute-done.10.refs_3_), custom_call_target="tpu_custom_call" | custom-call | flops 786432 | bytes 2621440 | tf_op jit(solution)/shard_map/add/pallas_call | solution.py:342
  149.9 8.5 %all-to-all-start.3 = ((bf16[32,16,512]{2,1,0:T(8,128)(2,1)}), bf16[32,16,512]{2,1,0:T(8,128)(2,1)}, u32[]{:S(2)}, u32[]{:S(2)}) async-start(bf16[32,16,512]{2,1,0:T(8,128)(2,1)} %bitcast.18), calls=%async_computation.3 | async-start | bytes 1048576 | tf_op jit(solution)/shard_map/all_to_all | solution.py:380
  158.4 2.5 %unpack.1 = (bf16[1,256,2048]{2,1,0:T(8,128)(2,1)}, bf16[1,256,2048]{2,1,0:T(8,128)(2,1)}, bf16[1,256,2048]{2,1,0:T(8,128)(2,1)}) custom-call(bf16[16,768,128]{2,1,0:T(8,128)(2,1)S(1)} %all-to-all-done.2.src), custom_call_target="tpu_custom_call" | custom-call | bytes 6291456 | tf_op jit(solution)/shard_map/unpack/pallas_call | solution.py:72
  161.0 9.3 %all-to-all-done.3.in_ref = bf16[32,16,512]{2,1,0:T(8,128)(2,1)} async-done(((bf16[32,16,512]{2,1,0:T(8,128)(2,1)}), bf16[32,16,512]{2,1,0:T(8,128)(2,1)}, u32[]{:S(2)}, u32[]{:S(2)}) %all-to-all-start.3) | async-done | bytes 524320 | tf_op jit(solution)/shard_map/all_to_all | solution.py:380
  170.2 1.8 %sum.1 = f32[16,2048]{1,0:T(8,128)} custom-call(bf16[32,16,512]{2,1,0:T(8,128)(2,1)} %all-to-all-done.3.in_ref), custom_call_target="tpu_custom_call" | custom-call | flops 262144 | bytes 524288 | tf_op jit(solution)/shard_map/sum/pallas_call | solution.py:367
  (32 shorter events, 6.5 us)
Async XLA Ops:
  5.0 50.5 %copy-start.1 = (s32[1,32,3]{1,0,2:T(1,128)S(1)}, s32[1,32,3]{1,0,2:T(1,128)}, u32[]{:S(2)}) copy-start(s32[1,32,3]{1,0,2:T(1,128)} %param.13) | copy-start | bytes 1156
  5.0 53.0 %copy-start = (s32[1,2]{1,0:T(1,128)S(1)}, s32[1,2]{1,0:T(1,128)}, u32[]{:S(2)}) copy-start(s32[1,2]{1,0:T(1,128)} %glob_ref.3) | copy-start | bytes 28
  49.9 27.6 %collective-permute-start = (bf16[1,256,2048]{2,1,0:T(8,128)(2,1)}, bf16[1,256,2048]{2,1,0:T(8,128)(2,1)}, u32[]{:S(2)}, u32[]{:S(2)}) collective-permute-start(bf16[1,256,2048]{2,1,0:T(8,128)(2,1)} %refs_0_.2), channel_id=1, source_target_pairs={{0,1},{1,0},{2,3},{3,2},{4,5},{5,4},{6,7},{7,6},{8,9},{9,8},{10,11... | collective-permute-start | bytes 3145736 | tf_op jit(solution)/shard_map/ppermute | solution.py:384
  51.3 26.2 %all-to-all-start.1 = ((bf16[16,256,128]{2,1,0:T(8,128)(2,1)}), bf16[16,256,128]{2,1,0:T(8,128)(2,1)}, u32[]{:S(2)}, u32[]{:S(2)}) async-start(bf16[16,256,128]{2,1,0:T(8,128)(2,1)} %get-tuple-element.41), calls=%async_computation.1 | async-start | bytes 2097152 | tf_op jit(solution)/shard_map/all_to_all | solution.py:380
  56.7 20.8 %collective-permute-start.1 = (bf16[1,96,2048]{2,1,0:T(8,128)(2,1)S(1)}, bf16[1,96,2048]{2,1,0:T(8,128)(2,1)}, u32[]{:S(2)}, u32[]{:S(2)}) collective-permute-start(bf16[1,96,2048]{2,1,0:T(8,128)(2,1)S(1)} %slice.6), channel_id=1, source_target_pairs={{0,2},{2,0},{1,3},{3,1},{4,6},{6,4},{5,7},{7,5},{8,10},{10,8},{9,1... | collective-permute-start | bytes 1179656 | tf_op jit(solution)/shard_map/ppermute | solution.py:384
  78.6 24.9 %collective-permute-start.2 = (bf16[1,160,2048]{2,1,0:T(8,128)(2,1)S(1)}, bf16[1,160,2048]{2,1,0:T(8,128)(2,1)S(1)}, u32[]{:S(2)}, u32[]{:S(2)}) collective-permute-start(bf16[1,160,2048]{2,1,0:T(8,128)(2,1)S(1)} %slice.7), channel_id=1, source_target_pairs={{0,2},{2,0},{1,3},{3,1},{4,6},{6,4},{5,7},{7,5},{8,10},{10,8},{9,1... | collective-permute-start | bytes 1966088 | tf_op jit(solution)/shard_map/ppermute | solution.py:384
  78.9 24.6 %collective-permute-start.4 = (bf16[1024,128]{1,0:T(8,128)(2,1)}, bf16[1024,128]{1,0:T(8,128)(2,1)S(1)}, u32[]{:S(2)}, u32[]{:S(2)}) collective-permute-start(bf16[1024,128]{1,0:T(8,128)(2,1)} %bitcast.21), channel_id=1, source_target_pairs={{0,4},{4,8},{8,12},{12,0},{1,5},{5,9},{9,13},{13,1},{2,6},{6,10},{... | collective-permute-start | bytes 786440 | tf_op jit(solution)/shard_map/ppermute | solution.py:384
  80.2 23.3 %collective-permute-start.5 = (bf16[1024,128]{1,0:T(8,128)(2,1)}, bf16[1024,128]{1,0:T(8,128)(2,1)S(1)}, u32[]{:S(2)}, u32[]{:S(2)}) collective-permute-start(bf16[1024,128]{1,0:T(8,128)(2,1)} %bitcast.20), channel_id=1, source_target_pairs={{0,8},{4,12},{8,0},{12,4},{1,9},{5,13},{9,1},{13,5},{2,10},{6,14},... | collective-permute-start | bytes 786440 | tf_op jit(solution)/shard_map/ppermute | solution.py:384
  82.8 20.7 %collective-permute-start.6 = (bf16[1024,128]{1,0:T(8,128)(2,1)}, bf16[1024,128]{1,0:T(8,128)(2,1)S(1)}, u32[]{:S(2)}, u32[]{:S(2)}) collective-permute-start(bf16[1024,128]{1,0:T(8,128)(2,1)} %bitcast.19), channel_id=1, source_target_pairs={{0,12},{4,0},{8,4},{12,8},{1,13},{5,1},{9,5},{13,9},{2,14},{6,2},{... | collective-permute-start | bytes 786440 | tf_op jit(solution)/shard_map/ppermute | solution.py:384
  83.8 19.7 %collective-permute-start.3 = (bf16[1,96,2048]{2,1,0:T(8,128)(2,1)}, bf16[1,96,2048]{2,1,0:T(8,128)(2,1)S(1)}, u32[]{:S(2)}, u32[]{:S(2)}) collective-permute-start(bf16[1,96,2048]{2,1,0:T(8,128)(2,1)} %collective-permute-done.1.refs_2_), channel_id=1, source_target_pairs={{0,1},{1,0},{2,3},{3,2},{4,5},{5,4},{6,7},{7,6},{8,9},{9,8},{10,11... | collective-permute-start | bytes 1179656 | tf_op jit(solution)/shard_map/ppermute | solution.py:384
  103.5 8.1 %copy-start.5 = (bf16[1024,128]{1,0:T(8,128)(2,1)}, bf16[1024,128]{1,0:T(8,128)(2,1)S(1)}, u32[]{:S(2)}) copy-start(bf16[1024,128]{1,0:T(8,128)(2,1)S(1)} %collective-permute-done.4.refs_7_) | copy-start | bytes 786436
  103.5 0.7 copy-start.6
  103.5 0.8 copy-start.7
  103.5 0.9 copy-start.4
  104.5 0.8 copy-start.2
  105.3 44.6 %all-to-all-start.2 = ((bf16[16,768,128]{2,1,0:T(8,128)(2,1)}), bf16[16,768,128]{2,1,0:T(8,128)(2,1)S(1)}, u32[]{:S(2)}, u32[]{:S(2)}) async-start(bf16[16,768,128]{2,1,0:T(8,128)(2,1)} %bitcast.17), calls=%async_computation.2 | async-start | bytes 6291456 | tf_op jit(solution)/shard_map/all_to_all | solution.py:380
  108.9 2.6 %collective-permute-start.7 = (bf16[1,160,2048]{2,1,0:T(8,128)(2,1)}, bf16[1,160,2048]{2,1,0:T(8,128)(2,1)S(1)}, u32[]{:S(2)}, u32[]{:S(2)}) collective-permute-start(bf16[1,160,2048]{2,1,0:T(8,128)(2,1)} %copy-done.2), channel_id=1, source_target_pairs={{0,1},{1,0},{2,3},{3,2},{4,5},{5,4},{6,7},{7,6},{8,9},{9,8},{10,11... | collective-permute-start | bytes 1966088 | tf_op jit(solution)/shard_map/ppermute | solution.py:384
  111.5 0.8 copy-start.3
  120.0 15.1 %collective-permute-start.8 = (bf16[512,512]{1,0:T(8,128)(2,1)}, bf16[512,512]{1,0:T(8,128)(2,1)}, u32[]{:S(2)}, u32[]{:S(2)}) collective-permute-start(bf16[512,512]{1,0:T(8,128)(2,1)} %get-tuple-element.65), channel_id=1, source_target_pairs={{0,32},{32,64},{64,96},{96,0},{1,33},{33,65},{65,97},{97,1},{2,34}... | collective-permute-start | bytes 1572872 | tf_op jit(solution)/shard_map/ppermute | solution.py:384
  121.3 26.1 %collective-permute-start.9 = (bf16[512,512]{1,0:T(8,128)(2,1)}, bf16[512,512]{1,0:T(8,128)(2,1)}, u32[]{:S(2)}, u32[]{:S(2)}) collective-permute-start(bf16[512,512]{1,0:T(8,128)(2,1)} %get-tuple-element.66), channel_id=1, source_target_pairs={{0,64},{32,96},{64,0},{96,32},{1,65},{33,97},{65,1},{97,33},{2,66}... | collective-permute-start | bytes 1572872 | tf_op jit(solution)/shard_map/ppermute | solution.py:384
  123.9 23.5 %collective-permute-start.10 = (bf16[512,512]{1,0:T(8,128)(2,1)}, bf16[512,512]{1,0:T(8,128)(2,1)}, u32[]{:S(2)}, u32[]{:S(2)}) collective-permute-start(bf16[512,512]{1,0:T(8,128)(2,1)} %get-tuple-element.67), channel_id=1, source_target_pairs={{0,96},{32,0},{64,32},{96,64},{1,97},{33,1},{65,33},{97,65},{2,98}... | collective-permute-start | bytes 1572872 | tf_op jit(solution)/shard_map/ppermute | solution.py:384
  149.9 20.3 %all-to-all-start.3 = ((bf16[32,16,512]{2,1,0:T(8,128)(2,1)}), bf16[32,16,512]{2,1,0:T(8,128)(2,1)}, u32[]{:S(2)}, u32[]{:S(2)}) async-start(bf16[32,16,512]{2,1,0:T(8,128)(2,1)} %bitcast.18), calls=%async_computation.3 | async-start | bytes 1048576 | tf_op jit(solution)/shard_map/all_to_all | solution.py:380

commit v3 on v2

v3 whole, which is shorter than its diff:
```python
import functools
import math

import jax
import jax.numpy as jnp
from jax import lax
from jax.experimental import pallas as pl
from jax.experimental.pallas import tpu as pltpu
from jax.sharding import Mesh, PartitionSpec as P

D = 128
BLOCK = 128
F32 = jnp.float32
BF16 = jnp.bfloat16
LOG2E = 1.4426950408889634
DP = ("y", "zh")
CTX = ("x", "zl", "core")
NEG = float("-inf")


def hbm(array):
    return pltpu.with_memory_space_constraint(array, pltpu.HBM)


def pack_kernel(pieces, *refs):
    ins, (out, bufs, sems) = refs[:-3], refs[-3:]
    count, rows = bufs.shape[:2]
    size = rows // pieces
    copies = {}
    for m in range(pieces):
        for n, src in enumerate(ins):
            at = pl.ds(m * size, size)
            copies[m, n] = pltpu.make_async_copy(src.at[0, at], bufs.at[n, at], sems.at[m, n])
            copies[m, n].start()
    for m in range(pieces):
        for n in range(count):
            copies[m, n].wait()
            first = n * rows + m * size
            for h in range(out.shape[0]):
                out[h, first : first + size, :] = bufs[
                    n, m * size : (m + 1) * size, h * D : (h + 1) * D
                ]


def pack(*arrays):
    rows, cols = arrays[0].shape[1:]
    heads, count, pieces = cols // D, len(arrays), 4
    return pl.pallas_call(
        functools.partial(pack_kernel, pieces),
        out_shape=jax.ShapeDtypeStruct((heads, count * rows, D), BF16),
        in_specs=[pl.BlockSpec(memory_space=pl.ANY)] * count,
        out_specs=pl.BlockSpec(memory_space=pltpu.VMEM),
        scratch_shapes=[
            pltpu.VMEM((count, rows, cols), BF16),
            pltpu.SemaphoreType.DMA((pieces, count)),
        ],
        compiler_params=pltpu.CompilerParams(vmem_limit_bytes=24 * 1024 * 1024),
        name="pack",
        cost_estimate=pl.CostEstimate(
            flops=0, bytes_accessed=4 * rows * cols * count, transcendentals=0
        ),
    )(*[hbm(a) for a in arrays])


def unpack_kernel(count, src, *outs):
    rows = outs[0].shape[1]
    for n, out in enumerate(outs):
        for h in range(src.shape[0]):
            out[0, :, h * D : (h + 1) * D] = src[h, n * rows : (n + 1) * rows, :]


def unpack(array, count):
    heads, rows = array.shape[0], array.shape[1] // count
    return pl.pallas_call(
        functools.partial(unpack_kernel, count),
        out_shape=[jax.ShapeDtypeStruct((1, rows, heads * D), BF16)] * count,
        in_specs=[pl.BlockSpec(memory_space=pltpu.VMEM)],
        out_specs=[pl.BlockSpec(memory_space=pltpu.VMEM)] * count,
        compiler_params=pltpu.CompilerParams(vmem_limit_bytes=24 * 1024 * 1024),
        name="unpack",
        cost_estimate=pl.CostEstimate(
            flops=0, bytes_accessed=4 * rows * heads * D * count, transcendentals=0
        ),
    )(array)


def table_row(glob_ref, rand_ref, b, nb):
    left, right = b - 1, b + 1
    g0, g1 = glob_ref[0, 0], glob_ref[0, 1]
    idx = [
        jnp.maximum(left, 0),
        b,
        jnp.minimum(right, nb - 1),
        g0,
        g1,
        rand_ref[0, b, 0],
        rand_ref[0, b, 1],
        rand_ref[0, b, 2],
    ]

    def bias(c):
        return jnp.where(c, 0.0, NEG).astype(F32)

    biases = [
        bias(left >= 0),
        None,
        bias(right < nb),
        bias(jnp.abs(g0 - b) > 1),
        bias(jnp.abs(g1 - b) > 1),
        None,
        None,
        None,
    ]
    return idx, biases


def nt(a, b):
    return lax.dot_general(a, b, (((1,), (1,)), ((), ())), preferred_element_type=F32)


def tn(a, b):
    return lax.dot_general(a, b, (((0,), (0,)), ((), ())), preferred_element_type=F32)


def diag(a, b):
    zero = jnp.zeros_like(a)
    return jnp.concatenate(
        [jnp.concatenate([a, zero], axis=1), jnp.concatenate([zero, b], axis=1)], axis=0
    )


def pick(ref, idx, kind):
    return jnp.concatenate([ref[i // 2, 2 * kind + i % 2] for i in idx], axis=0)


def two(ref, u, kind):
    return diag(ref[u, 2 * kind], ref[u, 2 * kind + 1])


def tile(array, j, half):
    return array[j * D : (j + 1) * D, half * D : (half + 1) * D]


def add_tiles(acc, idx_pair, part):
    for j in range(8):
        for half, idx in enumerate(idx_pair):
            acc[idx[j]] += tile(part, j, half)


Q, K, G, V = 0, 1, 2, 3
DQ, DK, DV = 0, 1, 2
UNROLL = 8
LOADS = 4


def probs_kernel(nx, scale, glob_ref, rand_ref, me_ref, in_hbm, p_ref, dv_ref, *rest):
    parts, (acc, buf, sems) = rest[:-3], rest[-3:]
    half_nb, nb = buf.shape[0], acc.shape[0]
    copies = []
    for kind in (K, Q, G):
        at = pl.ds(2 * kind, 2)
        for piece in range(LOADS):
            size = half_nb // LOADS
            rows = pl.ds(piece * size, size)
            copies.append(
                pltpu.make_async_copy(
                    in_hbm.at[rows, at], buf.at[rows, at], sems.at[kind * LOADS + piece]
                )
            )
            copies[-1].start()
    acc[...] = jnp.zeros_like(acc)
    for copy in copies:
        copy.wait()
    in_ref = buf

    def pair(u):
        rows = [table_row(glob_ref, rand_ref, 2 * u + half, nb) for half in range(2)]
        idx_pair = [row[0] for row in rows]
        keys = jnp.concatenate([pick(in_ref, idx, K) for idx in idx_pair], axis=1)
        s = nt(keys, two(in_ref, u, Q))
        ps = []
        for half, (_, biases) in enumerate(rows):
            tiles = [tile(s, j, half) for j in range(8)]
            tiles = [t if c is None else t + c for t, c in zip(tiles, biases)]
            top = jnp.max(functools.reduce(jnp.maximum, tiles), axis=0, keepdims=True)
            e = [jnp.exp2((t - top) * (scale * LOG2E)) for t in tiles]
            inv = 1.0 / jnp.sum(functools.reduce(jnp.add, e), axis=0, keepdims=True)
            ps.append(jnp.concatenate([(t * inv).astype(BF16) for t in e], axis=0))
        p = jnp.concatenate(ps, axis=1)
        p_ref[u] = p
        part = jnp.dot(p, two(in_ref, u, G), preferred_element_type=F32)
        add_tiles(acc, idx_pair, part)

    @pl.loop(0, half_nb // UNROLL)
    def _(step):
        for u in range(UNROLL):
            pair(step * UNROLL + u)

    dv_ref[...] = acc[...].astype(BF16).reshape(dv_ref.shape)
    size = parts[0].shape[0]
    for n, part in enumerate(parts):
        part[...] = dv_ref[pl.ds(lax.rem(me_ref[0] + n, nx) * size, size)]


def probs_call(glob, rand, me, qkgv, nx, scale):
    half = qkgv.shape[0]
    smem, vmem = pl.BlockSpec(memory_space=pltpu.SMEM), pl.BlockSpec(memory_space=pltpu.VMEM)
    return pl.pallas_call(
        functools.partial(probs_kernel, nx, scale),
        out_shape=[
            jax.ShapeDtypeStruct((half, 8 * BLOCK, 2 * BLOCK), BF16),
            jax.ShapeDtypeStruct((half, 2, BLOCK, D), BF16),
        ]
        + [pltpu.HBM((half // nx, 2, BLOCK, D), BF16)] * nx,
        in_specs=[smem, smem, smem, pl.BlockSpec(memory_space=pl.ANY)],
        out_specs=[vmem] * (2 + nx),
        scratch_shapes=[
            pltpu.VMEM((2 * half, BLOCK, D), F32),
            pltpu.VMEM((half, 6, BLOCK, D), BF16),
            pltpu.SemaphoreType.DMA((3 * LOADS,)),
        ],
        compiler_params=pltpu.CompilerParams(vmem_limit_bytes=24 * 1024 * 1024),
        name="probs",
        cost_estimate=pl.CostEstimate(
            flops=16 * half * 8 * BLOCK * BLOCK * D,
            bytes_accessed=14 * 1024 * 1024,
            transcendentals=2 * half * 8 * BLOCK * BLOCK,
        ),
    )(glob, rand, me, hbm(qkgv))


def grads_kernel(scale, glob_ref, rand_ref, in_ref, p_ref, dv_ref, out_ref, acc):
    half_nb, nb = in_ref.shape[0], acc.shape[0]
    acc[...] = jnp.zeros_like(acc)
    def pair(u):
        idx_pair = [table_row(glob_ref, rand_ref, 2 * u + half, nb)[0] for half in range(2)]
        vals = jnp.concatenate([pick(in_ref, idx, V) for idx in idx_pair], axis=1)
        dp = nt(vals, two(in_ref, u, G))
        both = []
        for half, idx in enumerate(idx_pair):
            ps = [tile(p_ref[u], j, half).astype(F32) for j in range(8)]
            ts = [ps[j] * tile(dp, j, half) for j in range(8)]
            delta = jnp.sum(functools.reduce(jnp.add, ts), axis=0, keepdims=True)
            ds = jnp.concatenate([(t - x * delta).astype(BF16) for t, x in zip(ts, ps)], axis=0)
            both.append(ds)
            out_ref[u, 2 * DQ + half] = (tn(ds, pick(in_ref, idx, K)) * scale).astype(BF16)
        ds = jnp.concatenate(both, axis=1)
        part = jnp.dot(ds, two(in_ref, u, Q), preferred_element_type=F32)
        add_tiles(acc, idx_pair, part)

    @pl.loop(0, half_nb // UNROLL)
    def _(step):
        for u in range(UNROLL):
            pair(step * UNROLL + u)

    out_ref[:, 2 * DK : 2 * DK + 2] = (acc[...] * scale).astype(BF16).reshape(dv_ref.shape)
    out_ref[:, 2 * DV : 2 * DV + 2] = dv_ref[...]


def grads_call(glob, rand, qkgv, p, dv, scale):
    half = qkgv.shape[0]
    smem, vmem = pl.BlockSpec(memory_space=pltpu.SMEM), pl.BlockSpec(memory_space=pltpu.VMEM)
    return pl.pallas_call(
        functools.partial(grads_kernel, scale),
        out_shape=pltpu.HBM((half, 6, BLOCK, D), BF16),
        in_specs=[smem, smem, vmem, vmem, vmem],
        out_specs=vmem,
        scratch_shapes=[pltpu.VMEM((2 * half, BLOCK, D), F32)],
        compiler_params=pltpu.CompilerParams(vmem_limit_bytes=24 * 1024 * 1024),
        name="grads",
        cost_estimate=pl.CostEstimate(
            flops=20 * half * 8 * BLOCK * BLOCK * D,
            bytes_accessed=14 * 1024 * 1024,
            transcendentals=0,
        ),
    )(glob, rand, qkgv, p, dv)


def weight_kernel(count, nx, nz, ny, me_ref, *refs):
    xs, parts, refs = refs[:count], refs[count : count + nx], refs[count + nx :]
    outs, (x_buf, cols, bufs, in_sems, x_sems, out_sems) = refs[:ny], refs[ny:]
    rows, size = cols.shape[0] // nz, bufs.shape[1]
    loads = []
    for n, part in enumerate(parts):
        head = pl.multiple_of(lax.rem(me_ref[0] + nx - n, nx) * D, D)
        for m in range(nz):
            first = pl.multiple_of((me_ref[1] ^ m) * rows, rows)
            loads.append(
                pltpu.make_async_copy(
                    part.at[pl.ds(first, rows)],
                    cols.at[pl.ds(m * rows, rows), pl.ds(head, D)],
                    in_sems.at[n * nz + m],
                )
            )
            loads[-1].start()
    x_loads = []
    for n in range(ny):
        at = pl.ds(pl.multiple_of(lax.rem(me_ref[2] + n, ny) * size, size), size)
        for m, x in enumerate(xs):
            load = pltpu.make_async_copy(
                x.at[0, :, at], x_buf.at[n, pl.ds(m * rows, rows)], x_sems.at[n * count + m]
            )
            load.start()
            x_loads.append(load)
    for load in loads:
        load.wait()
    stores = []
    for n, out in enumerate(outs):
        for load in x_loads[n * count : (n + 1) * count]:
            load.wait()
        bufs[n] = tn(x_buf[n], cols[...]).astype(BF16)
        stores.append(pltpu.make_async_copy(bufs.at[n], out, out_sems.at[n]))
        stores[n].start()
    for store in stores:
        store.wait()


def weight_call(me, xs, parts, nz, ny):
    nx, tokens = len(parts), parts[0].shape[0]
    features = xs[0].shape[2]
    size = features // ny
    smem, hbm_spec = pl.BlockSpec(memory_space=pltpu.SMEM), pl.BlockSpec(memory_space=pl.ANY)
    return pl.pallas_call(
        functools.partial(weight_kernel, len(xs), nx, nz, ny),
        out_shape=[pltpu.HBM((size, nx * D), BF16)] * ny,
        in_specs=[smem] + [hbm_spec] * (len(xs) + nx),
        out_specs=[hbm_spec] * ny,
        scratch_shapes=[
            pltpu.VMEM((ny, tokens, size), BF16),
            pltpu.VMEM((tokens, nx * D), BF16),
            pltpu.VMEM((ny, size, nx * D), BF16),
            pltpu.SemaphoreType.DMA((nx * nz,)),
            pltpu.SemaphoreType.DMA((ny * len(xs),)),
            pltpu.SemaphoreType.DMA((ny,)),
        ],
        compiler_params=pltpu.CompilerParams(vmem_limit_bytes=24 * 1024 * 1024),
        name="weight",
        cost_estimate=pl.CostEstimate(
            flops=2 * tokens * features * nx * D,
            bytes_accessed=7 * 1024 * 1024,
            transcendentals=0,
        ),
    )(me, *[hbm(x) for x in xs], *[hbm(part) for part in parts])


def sum_kernel(nz, nx, scale, in_ref, out_ref):
    for n in range(nz):
        total = in_ref[n].astype(F32)
        for r in range(1, in_ref.shape[0] // nz):
            total = total + in_ref[r * nz + n].astype(F32)
        total = total * scale
        for h in range(nx):
            c = (h * nz + n) * D
            out_ref[:, c : c + D] = total[:, h * D : (h + 1) * D]


def sum_call(array, nz, nx, scale):
    rows = array.shape[1]
    return pl.pallas_call(
        functools.partial(sum_kernel, nz, nx, scale),
        out_shape=jax.ShapeDtypeStruct((rows, nz * nx * D), F32),
        in_specs=[pl.BlockSpec(memory_space=pltpu.VMEM)],
        out_specs=pl.BlockSpec(memory_space=pltpu.VMEM),
        name="sum",
        cost_estimate=pl.CostEstimate(
            flops=array.size, bytes_accessed=2 * array.size, transcendentals=0
        ),
    )(array)


def swap(array, axes):
    return lax.all_to_all(array, axes, split_axis=0, concat_axis=0, tiled=True)


def shift(array, axis, n, size):
    return lax.ppermute(array, axis, [(i, (i + n) % size) for i in range(size)])


def per_device(queries, keys, values, out_grad, layer_input, global_blocks, random_blocks):
    local, features = layer_input.shape[1:]
    n_ctx, n_dp = lax.axis_size(CTX), lax.axis_size(DP)
    nx, ny, nz = lax.axis_size("x"), lax.axis_size("y"), lax.axis_size(("zl", "core"))
    nr = lax.axis_size(("zh", "x"))
    doc = local * n_ctx
    nb = doc // BLOCK
    scale = 1.0 / math.sqrt(D)
    me = [lax.axis_index("x"), lax.axis_index(("zl", "core")), lax.axis_index("y")]
    me = jnp.stack(me).astype(jnp.int32)

    qkgv = swap(pack(queries, keys, out_grad, values), CTX)
    qkgv, x_own = lax.optimization_barrier((qkgv, layer_input))
    qkgv = qkgv.reshape(n_ctx, 8, BLOCK, D)
    x_zl = shift(x_own, "zl", 1, 2)
    x_core = shift(x_own, "core", 1, 2)
    probs, dv, *parts = probs_call(global_blocks, random_blocks, me, qkgv, nx, scale)
    parts = [part.reshape(doc // nx, D) for part in parts]
    parts = parts[:1] + [shift(parts[n], "x", n, nx) for n in range(1, nx)]
    qkv = grads_call(global_blocks, random_blocks, qkgv, probs, dv, scale)
    qkv, x_zl, x_core, *parts = lax.optimization_barrier((qkv, x_zl, x_core, *parts))
    back = swap(qkv.reshape(n_ctx, 3 * local, D), CTX)
    xs = [x_own, x_core, x_zl, shift(x_zl, "core", 1, 2)]
    w_parts = weight_call(me, xs, parts, nz, ny)
    w_parts = [w_parts[0]] + [shift(w_parts[n], "y", n, ny) for n in range(1, ny)]
    w_y = sum(part.astype(F32) for part in w_parts).astype(BF16)

    rows = features // (n_dp * n_ctx)
    w_y, back = lax.optimization_barrier((w_y, back))
    w_all = swap(w_y.reshape(nr * nz, rows, nx * D), ("zh", "x", "zl", "core"))
    w_out = sum_call(w_all, nz, nx, 1.0 / math.sqrt(doc * n_dp))
    dq, dk, dv_out = unpack(back, 3)
    return (dq, dk, dv_out, w_out)


def solution(mesh):
    fine = Mesh(mesh.devices.reshape(4, 2, 4, 2, 2), DP + CTX)
    tokens = P(DP, CTX, None)
    return jax.shard_map(
        per_device,
        mesh=fine,
        in_specs=(tokens,) * 5 + (P(DP, None), P(DP, None, None)),
        out_specs=(tokens, tokens, tokens, P(DP + CTX, None)),
        check_vma=False,
    )
```

time: 173 us -> 164 us (0.948)
  blocking collectives: 44.9 us -> 56.2 us
  Pallas kernels: 51.4 us -> 42.4 us
  starting transfers between devices: 31.5 us -> 22.6 us
  local copies, waits for them, and re-layouts: 4.87 us -> 2.18 us
  other arithmetic: 0.08 us -> 2.18 us
    all_to_all x1, blocking collectives: 44.9 us -> 56.2 us  [swap(): return lax.all_to_all(array, axes, split_axis=0, concat_axis=0, tiled=True)]
    pallas_call x5 -> x4, Pallas kernels: 47.1 us -> 38.1 us  [the longest x1 15.2 us: grads_call(): pl.pallas_call(functools.partial(grads_kernel, scale), out_shape=pltpu.HB...]
    ppermute x11 -> x9, starting transfers between devices: 15.1 us -> 8.98 us  [shift(): return lax.ppermute(array, axis, [(i, (i + n) % size) for i in range(size)])]
    all_to_all x3 -> x2, starting transfers between devices: 16.4 us -> 13.6 us  [swap(): return lax.all_to_all(array, axes, split_axis=0, concat_axis=0, tiled=True)]
    slice x2 -> x0, local copies, waits for them, and re-layouts: 2.16 us -> none  [the longest x1 1.14 us: per_device(): x_zl.append(shift(x_own[:, cut:], 'zl', 1, 2))]
    convert_element_type x0 -> x1, other arithmetic: none -> 2.11 us  [per_device(): w_y = sum((part.astype(F32) for part in w_parts)).astype(BF16)]
    ppermute x11 -> x9, waiting for transfers between devices: 29.3 us -> 28.5 us  [shift(): return lax.ppermute(array, axis, [(i, (i + n) % size) for i in range(size)])]
    all_to_all x3 -> x2, waiting for transfers between devices: 9.27 us -> 9.27 us  [swap(): return lax.all_to_all(array, axes, split_axis=0, concat_axis=0, tiled=True)]
  transfers between devices with their start and end apart: 14 -> 11, of which waited for: 5 -> 4; matrix products, arithmetic and copies ran while one was open for 1% -> 1% of each run, Pallas kernels for 26% -> 23%
where the time goes in v3:
time: 164 us
  blocking collectives  56.2 us (34%)
  Pallas kernels  42.4 us (26%)
  waiting for transfers between devices  37.7 us (23%)
  starting transfers between devices  22.6 us (14%)
  local copies, waits for them, and re-layouts  2.18 us (1%)
  other arithmetic  2.18 us (1%)
    all_to_all x1, blocking collectives, swap(): return lax.all_to_all(array, axes, split_axis=0, concat_axis=0, tiled=True)  56.2 us
    ppermute x9, waiting for transfers between devices, shift(): return lax.ppermute(array, axis, [(i, (i + n) % size) for i in range(size)])  28.5 us
    pallas_call x1, Pallas kernels, grads_call(): pl.pallas_call(functools.partial(grads_kernel, scale), out_shape=pltpu.HB...  15.2 us
    pallas_call x1, Pallas kernels, probs_call(): pl.pallas_call(functools.partial(probs_kernel, nx, scale), out_shape=[jax...  13.6 us
    all_to_all x2, starting transfers between devices, swap(): return lax.all_to_all(array, axes, split_axis=0, concat_axis=0, tiled=True)  13.6 us
    all_to_all x2, waiting for transfers between devices, swap(): return lax.all_to_all(array, axes, split_axis=0, concat_axis=0, tiled=True)  9.27 us
    ppermute x9, starting transfers between devices, shift(): return lax.ppermute(array, axis, [(i, (i + n) % size) for i in range(size)])  8.98 us
    pallas_call x1, Pallas kernels, weight_call(): pl.pallas_call(functools.partial(weight_kernel, len(xs), nx, nz, ny), out...  6.93 us
  transfers between devices with their start and end apart: 11, of which 4 were waited for; matrix products, arithmetic and copies ran while one was open for 1% of the time, Pallas kernels for 23%

profile of v3, /device:TPU:1, one launch (start us, length us, event | category | flops | bytes accessed | tf_op | source)
XLA Modules:
  0.0 164.0 jit_solution(176372429587057755)
XLA Ops:
  0.6 2.3 %pack.1 = bf16[16,1024,128]{2,1,0:T(8,128)(2,1)S(1)} custom-call(bf16[1,256,2048]{2,1,0:T(8,128)(2,1)} %refs_0_.1, bf16[1,256,2048]{2,1,0:T(8,128)(2,1)} %refs_1_.1, bf16[1,256,2048]{2,1,0:T(8,128)(2,1)} %refs_2_.1, bf16[1,256,2048]{2,1,0:T(8,128)(2,1)} %refs_3_.1), custom_call_target="tpu_custom_call" | custom-call | bytes 8388608 | tf_op jit(solution)/shard_map/pack/pallas_call | solution.py:48
  3.0 56.2 %all_to_all.15 = bf16[16,1024,128]{2,1,0:T(8,128)(2,1)} all-to-all(bf16[16,1024,128]{2,1,0:T(8,128)(2,1)S(1)} %pack.1), channel_id=1, replica_groups=mesh['y'=4,'zh'=2,'x'=4,'zl'=2,'core'=2] {'x','zl','core'}, dimensions={0} | all-to-all | bytes 8388608 | tf_op jit(solution)/shard_map/all_to_all | solution.py:372
  59.2 1.2 collective-permute-start
  60.4 0.5 collective-permute-start.1
  61.0 13.6 %probs.1 = (bf16[16,1024,256]{2,1,0:T(8,128)(2,1)S(1)}, bf16[16,2,128,128]{3,2,1,0:T(8,128)(2,1)S(1)}, bf16[4,2,128,128]{3,2,1,0:T(8,128)(2,1)}, bf16[4,2,128,12...) custom-call(s32[1,2]{1,0:T(1,128)S(1)} %copy-done.1, ...), custom_call_target="tpu_custom_call" | custom-call | flops 4294967296 | bytes 14680064 | tf_op jit(solution)/shard_map/probs/pallas_call | solution.py:208
  74.8 1.6 collective-permute-start.3
  76.4 1.6 collective-permute-start.4
  78.0 15.2 %grads.1 = bf16[16,6,128,128]{3,2,1,0:T(8,128)(2,1)} custom-call(s32[1,2]{1,0:T(1,128)S(1)} %copy-done.1, s32[1,32,3]{2,1,0:T(8,128)S(1)} %copy.12.rand_ref, bf16[16,8,128,128]{3,2,1,0:T(8,128)(2,1)S(1)} %bitcast.11, bf16[16,1024,256]{2,1,0:T(8,128)(2,1)S(1)} %get-tuple-element.30.p_ref, bf16[16,2,128,128]{3,2,1,0:T(8,128)(2,1)S(1)} %get-tuple-element.31.dv_ref), custom_call_target="tpu_custom_call" | custom-call | flops 5368709120 | bytes 14680064 | tf_op jit(solution)/shard_map/grads/pallas_call | solution.py:263
  93.2 0.7 copy-done.7
  94.0 0.3 copy-done.4
  94.3 5.3 %all-to-all-start.1 = ((bf16[16,768,128]{2,1,0:T(8,128)(2,1)}), bf16[16,768,128]{2,1,0:T(8,128)(2,1)S(1)}, u32[]{:S(2)}, u32[]{:S(2)}) async-start(bf16[16,768,128]{2,1,0:T(8,128)(2,1)} %bitcast.12), calls=%async_computation.1 | async-start | bytes 6291456 | tf_op jit(solution)/shard_map/all_to_all | solution.py:372
  99.8 2.7 %collective-permute-done.5.refs_3_ = bf16[1,256,2048]{2,1,0:T(8,128)(2,1)S(1)} collective-permute-done((bf16[1,256,2048]{2,1,0:T(8,128)(2,1)}, bf16[1,256,2048]{2,1,0:T(8,128)(2,1)S(1)}, u32[]{:S(2)}, u32[]{:S(2)}) %collective-permute-start.5) | collective-permute-done | bytes 1048608 | tf_op jit(solution)/shard_map/ppermute | solution.py:376
  102.5 1.0 copy-done.5
  103.5 6.9 %weight.1 = (bf16[512,512]{1,0:T(8,128)(2,1)}, bf16[512,512]{1,0:T(8,128)(2,1)}, bf16[512,512]{1,0:T(8,128)(2,1)}, bf16[512,512]{1,0:T(8,128)(2,1)}) custom-call(s32[3]{0:T(128)S(1)} %pad_add_fusion.me_ref, bf16[1,256,2048]{2,1,0:T(8,128)(2,1)} %refs_0_.2, bf16[1,256,2048]{2,1,0:T(8,128)(2,1)} %copy-done.4, ...), custom_call_target="tpu_custom_call" | custom-call | flops 2147483648 | bytes 7340032 | tf_op jit(solution)/shard_map/weight/pallas_call | solution.py:323
  110.4 2.8 %collective-permute-start.8 = (bf16[512,512]{1,0:T(8,128)(2,1)}, bf16[512,512]{1,0:T(8,128)(2,1)S(1)}, u32[]{:S(2)}, u32[]{:S(2)}) collective-permute-start(bf16[512,512]{1,0:T(8,128)(2,1)} %get-tuple-element.45), channel_id=1, source_target_pairs={{0,96},{32,0},{64,32},{96,64},{1,97},{33,1},{65,33},{97,65},{2,98}... | collective-permute-start | bytes 1572872 | tf_op jit(solution)/shard_map/ppermute | solution.py:376
  113.2 0.4 collective-permute-start.7
  113.6 0.7 collective-permute-start.6
  114.2 21.4 %collective-permute-done.8 = bf16[512,512]{1,0:T(8,128)(2,1)S(1)} collective-permute-done((bf16[512,512]{1,0:T(8,128)(2,1)}, bf16[512,512]{1,0:T(8,128)(2,1)S(1)}, u32[]{:S(2)}, u32[]{:S(2)}) %collective-permute-start.8) | collective-permute-done | bytes 524320 | tf_op jit(solution)/shard_map/ppermute | solution.py:376
  135.7 4.3 %collective-permute-done.6 = bf16[512,512]{1,0:T(8,128)(2,1)S(1)} collective-permute-done((bf16[512,512]{1,0:T(8,128)(2,1)}, bf16[512,512]{1,0:T(8,128)(2,1)S(1)}, u32[]{:S(2)}, u32[]{:S(2)}) %collective-permute-start.6) | collective-permute-done | bytes 524320 | tf_op jit(solution)/shard_map/ppermute | solution.py:376
  140.0 2.1 %add_convert_fusion = bf16[512,512]{1,0:T(8,128)(2,1)} fusion(bf16[512,512]{1,0:T(8,128)(2,1)S(1)} %collective-permute-done.8, bf16[512,512]{1,0:T(8,128)(2,1)S(1)} %collective-permute-done.7, bf16[512,512]{1,0:T(8,128)(2,1)S(1)} %collective-permute-done.6, bf16[512,512]{1,0:T(8,128)(2,1)} %get-tuple-element.42), kind=kLoop, calls=%fused_computation | loop fusion | flops 2097152 | bytes 2621440 | tf_op jit(solution)/shard_map/convert_element_type | solution.py:404
  142.1 8.3 %all-to-all-start.2 = ((bf16[32,16,512]{2,1,0:T(8,128)(2,1)}), bf16[32,16,512]{2,1,0:T(8,128)(2,1)}, u32[]{:S(2)}, u32[]{:S(2)}) async-start(bf16[32,16,512]{2,1,0:T(8,128)(2,1)} %bitcast.13), calls=%async_computation.2 | async-start | bytes 1048576 | tf_op jit(solution)/shard_map/all_to_all | solution.py:372
  150.4 2.5 %unpack.1 = (bf16[1,256,2048]{2,1,0:T(8,128)(2,1)}, bf16[1,256,2048]{2,1,0:T(8,128)(2,1)}, bf16[1,256,2048]{2,1,0:T(8,128)(2,1)}) custom-call(bf16[16,768,128]{2,1,0:T(8,128)(2,1)S(1)} %all-to-all-done.1.src), custom_call_target="tpu_custom_call" | custom-call | bytes 6291456 | tf_op jit(solution)/shard_map/unpack/pallas_call | solution.py:74
  153.0 9.3 %all-to-all-done.2.in_ref = bf16[32,16,512]{2,1,0:T(8,128)(2,1)} async-done(((bf16[32,16,512]{2,1,0:T(8,128)(2,1)}), bf16[32,16,512]{2,1,0:T(8,128)(2,1)}, u32[]{:S(2)}, u32[]{:S(2)}) %all-to-all-start.2) | async-done | bytes 524320 | tf_op jit(solution)/shard_map/all_to_all | solution.py:372
  162.2 1.8 %sum.1 = f32[16,2048]{1,0:T(8,128)} custom-call(bf16[32,16,512]{2,1,0:T(8,128)(2,1)} %all-to-all-done.2.in_ref), custom_call_target="tpu_custom_call" | custom-call | flops 262144 | bytes 524288 | tf_op jit(solution)/shard_map/sum/pallas_call | solution.py:359
  (26 shorter events, 0.6 us)
Async XLA Ops:
  3.0 56.2 %copy-start.3 = (bf16[1,256,2048]{2,1,0:T(8,128)(2,1)S(1)}, bf16[1,256,2048]{2,1,0:T(8,128)(2,1)}, u32[]{:S(2)}) copy-start(bf16[1,256,2048]{2,1,0:T(8,128)(2,1)} %refs_0_.2) | copy-start | bytes 3145732
  3.0 57.9 %copy-start.2 = (s32[1,32,3]{1,0,2:T(1,128)S(1)}, s32[1,32,3]{1,0,2:T(1,128)}, u32[]{:S(2)}) copy-start(s32[1,32,3]{1,0,2:T(1,128)} %param.13) | copy-start | bytes 1156
  3.0 58.0 %copy-start.1 = (s32[1,2]{1,0:T(1,128)S(1)}, s32[1,2]{1,0:T(1,128)}, u32[]{:S(2)}) copy-start(s32[1,2]{1,0:T(1,128)} %glob_ref.3) | copy-start | bytes 28
  59.2 34.0 %collective-permute-start = (bf16[1,256,2048]{2,1,0:T(8,128)(2,1)S(1)}, bf16[1,256,2048]{2,1,0:T(8,128)(2,1)}, u32[]{:S(2)}, u32[]{:S(2)}) collective-permute-start(bf16[1,256,2048]{2,1,0:T(8,128)(2,1)S(1)} %copy-done.3), channel_id=1, source_target_pairs={{0,2},{2,0},{1,3},{3,1},{4,6},{6,4},{5,7},{7,5},{8,10},{10,8},{9,1... | collective-permute-start | bytes 3145736 | tf_op jit(solution)/shard_map/ppermute | solution.py:376
  60.4 32.8 %collective-permute-start.1 = (bf16[1,256,2048]{2,1,0:T(8,128)(2,1)S(1)}, bf16[1,256,2048]{2,1,0:T(8,128)(2,1)S(1)}, u32[]{:S(2)}, u32[]{:S(2)}) collective-permute-start(bf16[1,256,2048]{2,1,0:T(8,128)(2,1)S(1)} %copy-done.3), channel_id=1, source_target_pairs={{0,1},{1,0},{2,3},{3,2},{4,5},{5,4},{6,7},{7,6},{8,9},{9,8},{10,11... | collective-permute-start | bytes 3145736 | tf_op jit(solution)/shard_map/ppermute | solution.py:376
  61.0 16.9 %copy-start = (bf16[16,1024,128]{2,1,0:T(8,128)(2,1)S(1)}, bf16[16,1024,128]{2,1,0:T(8,128)(2,1)}, u32[]{:S(2)}) copy-start(bf16[16,1024,128]{2,1,0:T(8,128)(2,1)} %all_to_all.15) | copy-start | bytes 12582916
  74.7 18.5 %collective-permute-start.2 = (bf16[1024,128]{1,0:T(8,128)(2,1)}, bf16[1024,128]{1,0:T(8,128)(2,1)S(1)}, u32[]{:S(2)}, u32[]{:S(2)}) collective-permute-start(bf16[1024,128]{1,0:T(8,128)(2,1)} %bitcast.16), channel_id=1, source_target_pairs={{0,4},{4,8},{8,12},{12,0},{1,5},{5,9},{9,13},{13,1},{2,6},{6,10},{... | collective-permute-start | bytes 786440 | tf_op jit(solution)/shard_map/ppermute | solution.py:376
  74.8 18.4 %collective-permute-start.3 = (bf16[1024,128]{1,0:T(8,128)(2,1)}, bf16[1024,128]{1,0:T(8,128)(2,1)S(1)}, u32[]{:S(2)}, u32[]{:S(2)}) collective-permute-start(bf16[1024,128]{1,0:T(8,128)(2,1)} %bitcast.15), channel_id=1, source_target_pairs={{0,8},{4,12},{8,0},{12,4},{1,9},{5,13},{9,1},{13,5},{2,10},{6,14},... | collective-permute-start | bytes 786440 | tf_op jit(solution)/shard_map/ppermute | solution.py:376
  76.4 16.8 %collective-permute-start.4 = (bf16[1024,128]{1,0:T(8,128)(2,1)}, bf16[1024,128]{1,0:T(8,128)(2,1)S(1)}, u32[]{:S(2)}, u32[]{:S(2)}) collective-permute-start(bf16[1024,128]{1,0:T(8,128)(2,1)} %bitcast.14), channel_id=1, source_target_pairs={{0,12},{4,0},{8,4},{12,8},{1,13},{5,1},{9,5},{13,9},{2,14},{6,2},{... | collective-permute-start | bytes 786440 | tf_op jit(solution)/shard_map/ppermute | solution.py:376
  93.1 9.4 %copy-start.6 = (bf16[1024,128]{1,0:T(8,128)(2,1)}, bf16[1024,128]{1,0:T(8,128)(2,1)S(1)}, u32[]{:S(2)}) copy-start(bf16[1024,128]{1,0:T(8,128)(2,1)S(1)} %collective-permute-done.2.refs_5_) | copy-start | bytes 786436
  93.2 0.8 copy-start.7
  93.2 0.8 copy-start.8
  93.2 1.1 copy-start.4
  94.3 47.8 %all-to-all-start.1 = ((bf16[16,768,128]{2,1,0:T(8,128)(2,1)}), bf16[16,768,128]{2,1,0:T(8,128)(2,1)S(1)}, u32[]{:S(2)}, u32[]{:S(2)}) async-start(bf16[16,768,128]{2,1,0:T(8,128)(2,1)} %bitcast.12), calls=%async_computation.1 | async-start | bytes 6291456 | tf_op jit(solution)/shard_map/all_to_all | solution.py:372
  99.6 2.9 %collective-permute-start.5 = (bf16[1,256,2048]{2,1,0:T(8,128)(2,1)}, bf16[1,256,2048]{2,1,0:T(8,128)(2,1)S(1)}, u32[]{:S(2)}, u32[]{:S(2)}) collective-permute-start(bf16[1,256,2048]{2,1,0:T(8,128)(2,1)} %collective-permute-done.refs_2_), channel_id=1, source_target_pairs={{0,1},{1,0},{2,3},{3,2},{4,5},{5,4},{6,7},{7,6},{8,9},{9,8},{10,11... | collective-permute-start | bytes 3145736 | tf_op jit(solution)/shard_map/ppermute | solution.py:376
  102.5 1.0 copy-start.5
  110.4 25.2 %collective-permute-start.8 = (bf16[512,512]{1,0:T(8,128)(2,1)}, bf16[512,512]{1,0:T(8,128)(2,1)S(1)}, u32[]{:S(2)}, u32[]{:S(2)}) collective-permute-start(bf16[512,512]{1,0:T(8,128)(2,1)} %get-tuple-element.45), channel_id=1, source_target_pairs={{0,96},{32,0},{64,32},{96,64},{1,97},{33,1},{65,33},{97,65},{2,98}... | collective-permute-start | bytes 1572872 | tf_op jit(solution)/shard_map/ppermute | solution.py:376
  113.2 22.5 %collective-permute-start.7 = (bf16[512,512]{1,0:T(8,128)(2,1)}, bf16[512,512]{1,0:T(8,128)(2,1)S(1)}, u32[]{:S(2)}, u32[]{:S(2)}) collective-permute-start(bf16[512,512]{1,0:T(8,128)(2,1)} %get-tuple-element.44), channel_id=1, source_target_pairs={{0,64},{32,96},{64,0},{96,32},{1,65},{33,97},{65,1},{97,33},{2,66}... | collective-permute-start | bytes 1572872 | tf_op jit(solution)/shard_map/ppermute | solution.py:376
  113.6 26.4 %collective-permute-start.6 = (bf16[512,512]{1,0:T(8,128)(2,1)}, bf16[512,512]{1,0:T(8,128)(2,1)S(1)}, u32[]{:S(2)}, u32[]{:S(2)}) collective-permute-start(bf16[512,512]{1,0:T(8,128)(2,1)} %get-tuple-element.43), channel_id=1, source_target_pairs={{0,32},{32,64},{64,96},{96,0},{1,33},{33,65},{65,97},{97,1},{2,34}... | collective-permute-start | bytes 1572872 | tf_op jit(solution)/shard_map/ppermute | solution.py:376
  142.1 20.1 %all-to-all-start.2 = ((bf16[32,16,512]{2,1,0:T(8,128)(2,1)}), bf16[32,16,512]{2,1,0:T(8,128)(2,1)}, u32[]{:S(2)}, u32[]{:S(2)}) async-start(bf16[32,16,512]{2,1,0:T(8,128)(2,1)} %bitcast.13), calls=%async_computation.2 | async-start | bytes 1048576 | tf_op jit(solution)/shard_map/all_to_all | solution.py:372

commit v4 on v3

--- a/solution.py
+++ b/solution.py
@@ -18,41 +18,59 @@
 NEG = float("-inf")
 
 
+def vmem_pin(array):
+    return pltpu.with_memory_space_constraint(array, pltpu.VMEM)
+
+
 def hbm(array):
     return pltpu.with_memory_space_constraint(array, pltpu.HBM)
 
 
-def pack_kernel(pieces, *refs):
-    ins, (out, bufs, sems) = refs[:-3], refs[-3:]
+def pack_kernel(pieces, first_count, *refs):
+    ins, (out, late_hbm, bufs, late, sems, late_sem) = refs[:-6], refs[-6:]
     count, rows = bufs.shape[:2]
     size = rows // pieces
+    order = list(range(first_count, count)) + list(range(first_count))
     copies = {}
-    for m in range(pieces):
-        for n, src in enumerate(ins):
+    for n in order:
+        for m in range(pieces):
             at = pl.ds(m * size, size)
-            copies[m, n] = pltpu.make_async_copy(src.at[0, at], bufs.at[n, at], sems.at[m, n])
-            copies[m, n].start()
-    for m in range(pieces):
-        for n in range(count):
-            copies[m, n].wait()
-            first = n * rows + m * size
+            copies[n, m] = pltpu.make_async_copy(ins[n].at[0, at], bufs.at[n, at], sems.at[n, m])
+            copies[n, m].start()
+    leave = pltpu.make_async_copy(late, late_hbm, late_sem)
+    for n in order:
+        to, i = (late, n - first_count) if n >= first_count else (out, n)
+        for m in range(pieces):
+            copies[n, m].wait()
+            first = i * rows + m * size
             for h in range(out.shape[0]):
-                out[h, first : first + size, :] = bufs[
+                to[h, first : first + size, :] = bufs[
                     n, m * size : (m + 1) * size, h * D : (h + 1) * D
                 ]
-
-
-def pack(*arrays):
+        if n == count - 1:
+            leave.start()
+    leave.wait()
+
+
+def pack(now, later):
+    arrays = [*now, *later]
     rows, cols = arrays[0].shape[1:]
     heads, count, pieces = cols // D, len(arrays), 4
-    return pl.pallas_call(
-        functools.partial(pack_kernel, pieces),
-        out_shape=jax.ShapeDtypeStruct((heads, count * rows, D), BF16),
-        in_specs=[pl.BlockSpec(memory_space=pl.ANY)] * count,
-        out_specs=pl.BlockSpec(memory_space=pltpu.VMEM),
+    late_shape = (heads, len(later) * rows, D)
+    any_spec = pl.BlockSpec(memory_space=pl.ANY)
+    return pl.pallas_call(
+        functools.partial(pack_kernel, pieces, len(now)),
+        out_shape=[
+            jax.ShapeDtypeStruct((heads, len(now) * rows, D), BF16),
+            pltpu.HBM(late_shape, BF16),
+        ],
+        in_specs=[any_spec] * count,
+        out_specs=[pl.BlockSpec(memory_space=pltpu.VMEM), any_spec],
         scratch_shapes=[
             pltpu.VMEM((count, rows, cols), BF16),
-            pltpu.SemaphoreType.DMA((pieces, count)),
+            pltpu.VMEM(late_shape, BF16),
+            pltpu.SemaphoreType.DMA((count, pieces)),
+            pltpu.SemaphoreType.DMA,
         ],
         compiler_params=pltpu.CompilerParams(vmem_limit_bytes=24 * 1024 * 1024),
         name="pack",
@@ -147,14 +165,13 @@
             acc[idx[j]] += tile(part, j, half)
 
 
-Q, K, G, V = 0, 1, 2, 3
+Q, K, G = 0, 1, 2
 DQ, DK, DV = 0, 1, 2
-UNROLL = 8
 LOADS = 4
 
 
-def probs_kernel(nx, scale, glob_ref, rand_ref, me_ref, in_hbm, p_ref, dv_ref, *rest):
-    parts, (acc, buf, sems) = rest[:-3], rest[-3:]
+def probs_kernel(nx, scale, glob_ref, rand_ref, me_ref, in_hbm, p_hbm, dv_ref, *rest):
+    parts, (acc, buf, p_ref, sems, p_sems) = rest[:-5], rest[-5:]
     half_nb, nb = buf.shape[0], acc.shape[0]
     copies = []
     for kind in (K, Q, G):
@@ -173,6 +190,9 @@
         copy.wait()
     in_ref = buf
 
+    def store(u):
+        return pltpu.make_async_copy(p_ref.at[u], p_hbm.at[u], p_sems.at[u])
+
     def pair(u):
         rows = [table_row(glob_ref, rand_ref, 2 * u + half, nb) for half in range(2)]
         idx_pair = [row[0] for row in rows]
@@ -188,53 +208,64 @@
             ps.append(jnp.concatenate([(t * inv).astype(BF16) for t in e], axis=0))
         p = jnp.concatenate(ps, axis=1)
         p_ref[u] = p
+        store(u).start()
         part = jnp.dot(p, two(in_ref, u, G), preferred_element_type=F32)
         add_tiles(acc, idx_pair, part)
 
-    @pl.loop(0, half_nb // UNROLL)
-    def _(step):
-        for u in range(UNROLL):
-            pair(step * UNROLL + u)
-
+    for u in range(half_nb):
+        pair(u)
     dv_ref[...] = acc[...].astype(BF16).reshape(dv_ref.shape)
     size = parts[0].shape[0]
     for n, part in enumerate(parts):
         part[...] = dv_ref[pl.ds(lax.rem(me_ref[0] + n, nx) * size, size)]
-
-
-def probs_call(glob, rand, me, qkgv, nx, scale):
-    half = qkgv.shape[0]
+    for u in range(half_nb):
+        store(u).wait()
+
+
+def probs_call(glob, rand, me, qkg, nx, scale):
+    half = qkg.shape[0]
     smem, vmem = pl.BlockSpec(memory_space=pltpu.SMEM), pl.BlockSpec(memory_space=pltpu.VMEM)
     return pl.pallas_call(
         functools.partial(probs_kernel, nx, scale),
         out_shape=[
-            jax.ShapeDtypeStruct((half, 8 * BLOCK, 2 * BLOCK), BF16),
-            jax.ShapeDtypeStruct((half, 2, BLOCK, D), BF16),
+            pltpu.HBM((half, 8 * BLOCK, 2 * BLOCK), BF16),
+            pltpu.HBM((half, 2, BLOCK, D), BF16),
         ]
         + [pltpu.HBM((half // nx, 2, BLOCK, D), BF16)] * nx,
         in_specs=[smem, smem, smem, pl.BlockSpec(memory_space=pl.ANY)],
-        out_specs=[vmem] * (2 + nx),
+        out_specs=[pl.BlockSpec(memory_space=pl.ANY)] + [vmem] * (1 + nx),
         scratch_shapes=[
             pltpu.VMEM((2 * half, BLOCK, D), F32),
             pltpu.VMEM((half, 6, BLOCK, D), BF16),
+            pltpu.VMEM((half, 8 * BLOCK, 2 * BLOCK), BF16),
             pltpu.SemaphoreType.DMA((3 * LOADS,)),
+            pltpu.SemaphoreType.DMA((half,)),
         ],
-        compiler_params=pltpu.CompilerParams(vmem_limit_bytes=24 * 1024 * 1024),
+        compiler_params=pltpu.CompilerParams(vmem_limit_bytes=32 * 1024 * 1024),
         name="probs",
         cost_estimate=pl.CostEstimate(
             flops=16 * half * 8 * BLOCK * BLOCK * D,
             bytes_accessed=14 * 1024 * 1024,
             transcendentals=2 * half * 8 * BLOCK * BLOCK,
         ),
-    )(glob, rand, me, hbm(qkgv))
-
-
-def grads_kernel(scale, glob_ref, rand_ref, in_ref, p_ref, dv_ref, out_ref, acc):
+    )(glob, rand, me, hbm(qkg))
+
+
+def grads_kernel(scale, glob_ref, rand_ref, in_ref, v_ref, p_hbm, dv_hbm, out_ref, *rest):
+    acc, p_ref, sems = rest
     half_nb, nb = in_ref.shape[0], acc.shape[0]
+
+    def load(u):
+        return pltpu.make_async_copy(p_hbm.at[u], p_ref.at[u], sems.at[u])
+
+    for u in range(half_nb):
+        load(u).start()
+    dv_load = pltpu.make_async_copy(dv_hbm, out_ref.at[:, pl.ds(2 * DV, 2)], sems.at[half_nb])
+    dv_load.start()
     acc[...] = jnp.zeros_like(acc)
     def pair(u):
         idx_pair = [table_row(glob_ref, rand_ref, 2 * u + half, nb)[0] for half in range(2)]
-        vals = jnp.concatenate([pick(in_ref, idx, V) for idx in idx_pair], axis=1)
+        vals = jnp.concatenate([pick(v_ref, idx, 0) for idx in idx_pair], axis=1)
         dp = nt(vals, two(in_ref, u, G))
         both = []
         for half, idx in enumerate(idx_pair):
@@ -248,35 +279,47 @@
         part = jnp.dot(ds, two(in_ref, u, Q), preferred_element_type=F32)
         add_tiles(acc, idx_pair, part)
 
-    @pl.loop(0, half_nb // UNROLL)
+    quarter = half_nb // 4
+
+    def batch(first, size):
+        for u in range(size):
+            load(first + u).wait()
+        for u in range(size):
+            pair(first + u)
+
+    @pl.loop(0, 2)
     def _(step):
-        for u in range(UNROLL):
-            pair(step * UNROLL + u)
-
-    out_ref[:, 2 * DK : 2 * DK + 2] = (acc[...] * scale).astype(BF16).reshape(dv_ref.shape)
-    out_ref[:, 2 * DV : 2 * DV + 2] = dv_ref[...]
-
-
-def grads_call(glob, rand, qkgv, p, dv, scale):
-    half = qkgv.shape[0]
+        batch(step * quarter, quarter)
+
+    batch(2 * quarter, 2 * quarter)
+    out_ref[:, 2 * DK : 2 * DK + 2] = (acc[...] * scale).astype(BF16).reshape(dv_hbm.shape)
+    dv_load.wait()
+
+
+def grads_call(glob, rand, qkg, v, p, dv, scale):
+    half = qkg.shape[0]
     smem, vmem = pl.BlockSpec(memory_space=pltpu.SMEM), pl.BlockSpec(memory_space=pltpu.VMEM)
     return pl.pallas_call(
         functools.partial(grads_kernel, scale),
         out_shape=pltpu.HBM((half, 6, BLOCK, D), BF16),
-        in_specs=[smem, smem, vmem, vmem, vmem],
+        in_specs=[smem, smem, vmem, vmem] + [pl.BlockSpec(memory_space=pl.ANY)] * 2,
         out_specs=vmem,
-        scratch_shapes=[pltpu.VMEM((2 * half, BLOCK, D), F32)],
-        compiler_params=pltpu.CompilerParams(vmem_limit_bytes=24 * 1024 * 1024),
+        scratch_shapes=[
+            pltpu.VMEM((2 * half, BLOCK, D), F32),
+            pltpu.VMEM((half, 8 * BLOCK, 2 * BLOCK), BF16),
+            pltpu.SemaphoreType.DMA((half + 1,)),
+        ],
+        compiler_params=pltpu.CompilerParams(vmem_limit_bytes=32 * 1024 * 1024),
         name="grads",
         cost_estimate=pl.CostEstimate(
             flops=20 * half * 8 * BLOCK * BLOCK * D,
             bytes_accessed=14 * 1024 * 1024,
             transcendentals=0,
         ),
-    )(glob, rand, qkgv, p, dv)
-
-
-def weight_kernel(count, nx, nz, ny, me_ref, *refs):
+    )(glob, rand, qkg, v, hbm(p), hbm(dv))
+
+
+def weight_kernel(count, nx, nz, ny, offset, me_ref, *refs):
     xs, parts, refs = refs[:count], refs[count : count + nx], refs[count + nx :]
     outs, (x_buf, cols, bufs, in_sems, x_sems, out_sems) = refs[:ny], refs[ny:]
     rows, size = cols.shape[0] // nz, bufs.shape[1]
@@ -295,7 +338,8 @@
             loads[-1].start()
     x_loads = []
     for n in range(ny):
-        at = pl.ds(pl.multiple_of(lax.rem(me_ref[2] + n, ny) * size, size), size)
+        tile_size = xs[0].shape[2] // ny
+        at = pl.ds(pl.multiple_of(lax.rem(me_ref[2] + n, ny) * tile_size + offset, size), size)
         for m, x in enumerate(xs):
             load = pltpu.make_async_copy(
                 x.at[0, :, at], x_buf.at[n, pl.ds(m * rows, rows)], x_sems.at[n * count + m]
@@ -315,13 +359,13 @@
         store.wait()
 
 
-def weight_call(me, xs, parts, nz, ny):
+def weight_call(me, xs, parts, nz, ny, half):
     nx, tokens = len(parts), parts[0].shape[0]
     features = xs[0].shape[2]
-    size = features // ny
+    size = features // ny // 2
     smem, hbm_spec = pl.BlockSpec(memory_space=pltpu.SMEM), pl.BlockSpec(memory_space=pl.ANY)
     return pl.pallas_call(
-        functools.partial(weight_kernel, len(xs), nx, nz, ny),
+        functools.partial(weight_kernel, len(xs), nx, nz, ny, half * size),
         out_shape=[pltpu.HBM((size, nx * D), BF16)] * ny,
         in_specs=[smem] + [hbm_spec] * (len(xs) + nx),
         out_specs=[hbm_spec] * ny,
@@ -336,11 +380,11 @@
         compiler_params=pltpu.CompilerParams(vmem_limit_bytes=24 * 1024 * 1024),
         name="weight",
         cost_estimate=pl.CostEstimate(
-            flops=2 * tokens * features * nx * D,
-            bytes_accessed=7 * 1024 * 1024,
+            flops=tokens * features * nx * D,
+            bytes_accessed=4 * 1024 * 1024,
             transcendentals=0,
         ),
-    )(me, *[hbm(x) for x in xs], *[hbm(part) for part in parts])
+    )(me, *xs, *parts)
 
 
 def sum_kernel(nz, nx, scale, in_ref, out_ref):
@@ -387,21 +431,29 @@
     me = [lax.axis_index("x"), lax.axis_index(("zl", "core")), lax.axis_index("y")]
     me = jnp.stack(me).astype(jnp.int32)
 
-    qkgv = swap(pack(queries, keys, out_grad, values), CTX)
-    qkgv, x_own = lax.optimization_barrier((qkgv, layer_input))
-    qkgv = qkgv.reshape(n_ctx, 8, BLOCK, D)
+    qkg, v_in = pack((queries, keys, out_grad), (values,))
+    qkg = swap(qkg, CTX)
+    qkg, v_in, x_own = lax.optimization_barrier((qkg, v_in, layer_input))
+    v_in = swap(v_in, CTX).reshape(n_ctx, 2, BLOCK, D)
+    qkg = qkg.reshape(n_ctx, 6, BLOCK, D)
     x_zl = shift(x_own, "zl", 1, 2)
     x_core = shift(x_own, "core", 1, 2)
-    probs, dv, *parts = probs_call(global_blocks, random_blocks, me, qkgv, nx, scale)
+    probs, dv, *parts = probs_call(global_blocks, random_blocks, me, qkg, nx, scale)
+    v_in, *parts = lax.optimization_barrier((v_in, *parts))
     parts = [part.reshape(doc // nx, D) for part in parts]
     parts = parts[:1] + [shift(parts[n], "x", n, nx) for n in range(1, nx)]
-    qkv = grads_call(global_blocks, random_blocks, qkgv, probs, dv, scale)
+    qkv = grads_call(global_blocks, random_blocks, qkg, v_in, probs, dv, scale)
     qkv, x_zl, x_core, *parts = lax.optimization_barrier((qkv, x_zl, x_core, *parts))
     back = swap(qkv.reshape(n_ctx, 3 * local, D), CTX)
-    xs = [x_own, x_core, x_zl, shift(x_zl, "core", 1, 2)]
-    w_parts = weight_call(me, xs, parts, nz, ny)
-    w_parts = [w_parts[0]] + [shift(w_parts[n], "y", n, ny) for n in range(1, ny)]
-    w_y = sum(part.astype(F32) for part in w_parts).astype(BF16)
+    x_both = vmem_pin(shift(x_zl, "core", 1, 2))
+    xs = [hbm(x_own), hbm(x_core), hbm(x_zl), x_both]
+    parts = [hbm(part) for part in parts]
+    w_y = []
+    for half in range(2):
+        tiles = weight_call(me, xs, parts, nz, ny, half)
+        tiles = [tiles[0]] + [shift(tiles[n], "y", n, ny) for n in range(1, ny)]
+        w_y.append(sum(t.astype(F32) for t in tiles).astype(BF16))
+    w_y = jnp.concatenate(w_y, axis=0)
 
     rows = features // (n_dp * n_ctx)
     w_y, back = lax.optimization_barrier((w_y, back))

time: 164 us -> 161 us (0.982)
  starting transfers between devices: 22.6 us -> 34.1 us
  blocking collectives: 56.2 us -> 44.8 us
  waiting for transfers between devices: 37.7 us -> 29.6 us
  Pallas kernels: 42.4 us -> 47.8 us
    all_to_all x1, blocking collectives: 56.2 us -> 44.8 us  [swap(): return lax.all_to_all(array, axes, split_axis=0, concat_axis=0, tiled=True)]
    ppermute x9 -> x12, waiting for transfers between devices: 28.5 us -> 19.7 us  [shift(): return lax.ppermute(array, axis, [(i, (i + n) % size) for i in range(size)])]
    all_to_all x2 -> x3, starting transfers between devices: 13.6 us -> 19.8 us  [swap(): return lax.all_to_all(array, axes, split_axis=0, concat_axis=0, tiled=True)]
    ppermute x9 -> x12, starting transfers between devices: 8.98 us -> 14.3 us  [shift(): return lax.ppermute(array, axis, [(i, (i + n) % size) for i in range(size)])]
    pallas_call x1, Pallas kernels: 15.2 us -> 18 us  [grads_call(): pl.pallas_call(functools.partial(grads_kernel, scale), out_shape=pltpu.HB...]
    pallas_call x3 -> x4, Pallas kernels: 22.9 us -> 25.5 us  [the longest x1 13.4 us: probs_call(): pl.pallas_call(functools.partial(probs_kernel, nx, scale), out_shape=[plt...]
    all_to_all x2 -> x3, waiting for transfers between devices: 9.27 us -> 9.85 us  [swap(): return lax.all_to_all(array, axes, split_axis=0, concat_axis=0, tiled=True)]
  transfers between devices with their start and end apart: 11 -> 15, of which waited for: 4 -> 8; matrix products, arithmetic and copies ran while one was open for 1% -> 1% of each run, Pallas kernels for 23% -> 27%
where the time goes in v4:
time: 161 us; the launch traced here: 160 us
  Pallas kernels  47.8 us (30%)
  blocking collectives  44.8 us (28%)
  starting transfers between devices  34.1 us (21%)
  waiting for transfers between devices  29.6 us (18%)
  other arithmetic  2.14 us (1%)
    all_to_all x1, blocking collectives, swap(): return lax.all_to_all(array, axes, split_axis=0, concat_axis=0, tiled=True)  44.8 us
    all_to_all x3, starting transfers between devices, swap(): return lax.all_to_all(array, axes, split_axis=0, concat_axis=0, tiled=True)  19.8 us
    ppermute x12, waiting for transfers between devices, shift(): return lax.ppermute(array, axis, [(i, (i + n) % size) for i in range(size)])  19.7 us
    pallas_call x1, Pallas kernels, grads_call(): pl.pallas_call(functools.partial(grads_kernel, scale), out_shape=pltpu.HB...  18 us
    ppermute x12, starting transfers between devices, shift(): return lax.ppermute(array, axis, [(i, (i + n) % size) for i in range(size)])  14.3 us
    pallas_call x1, Pallas kernels, probs_call(): pl.pallas_call(functools.partial(probs_kernel, nx, scale), out_shape=[plt...  13.4 us
    all_to_all x3, waiting for transfers between devices, swap(): return lax.all_to_all(array, axes, split_axis=0, concat_axis=0, tiled=True)  9.85 us
    pallas_call x2, Pallas kernels, weight_call(): pl.pallas_call(functools.partial(weight_kernel, len(xs), nx, nz, ny, half...  9.74 us
  transfers between devices with their start and end apart: 15, of which 8 were waited for; matrix products, arithmetic and copies ran while one was open for 1% of the time, Pallas kernels for 27%

profile of v4, /device:TPU:1, one launch (start us, length us, event | category | flops | bytes accessed | tf_op | source)
XLA Modules:
  0.0 160.0 jit_solution(17180785646730844577)
XLA Ops:
  0.6 2.4 %pack.1 = (bf16[16,768,128]{2,1,0:T(8,128)(2,1)S(1)}, bf16[16,256,128]{2,1,0:T(8,128)(2,1)}) custom-call(bf16[1,256,2048]{2,1,0:T(8,128)(2,1)} %refs_0_.1, bf16[1,256,2048]{2,1,0:T(8,128)(2,1)} %refs_1_.1, bf16[1,256,2048]{2,1,0:T(8,128)(2,1)} %refs_2_.1, bf16[1,256,2048]{2,1,0:T(8,128)(2,1)} %refs_3_.1), custom_call_target="tpu_custom_call" | custom-call | bytes 8388608 | tf_op jit(solution)/shard_map/pack/pallas_call | solution.py:61
  3.0 44.8 %all_to_all.20 = bf16[16,768,128]{2,1,0:T(8,128)(2,1)} all-to-all(bf16[16,768,128]{2,1,0:T(8,128)(2,1)S(1)} %get-tuple-element.40), channel_id=1, replica_groups=mesh['y'=4,'zh'=2,'x'=4,'zl'=2,'core'=2] {'x','zl','core'}, dimensions={0} | all-to-all | bytes 6291456 | tf_op jit(solution)/shard_map/all_to_all | solution.py:416
  47.8 5.4 %all-to-all-start.1 = ((bf16[16,256,128]{2,1,0:T(8,128)(2,1)}), bf16[16,256,128]{2,1,0:T(8,128)(2,1)}, u32[]{:S(2)}, u32[]{:S(2)}) async-start(bf16[16,256,128]{2,1,0:T(8,128)(2,1)} %get-tuple-element.44), calls=%async_computation.1 | async-start | bytes 2097152 | tf_op jit(solution)/shard_map/all_to_all | solution.py:416
  53.2 1.4 collective-permute-start
  55.4 13.4 %probs.1 = (bf16[16,1024,256]{2,1,0:T(8,128)(2,1)}, bf16[16,2,128,128]{3,2,1,0:T(8,128)(2,1)}, bf16[4,2,128,128]{3,2,1,0:T(8,128)(2,1)}, bf16[4,2,128,128]{3,2,1...) custom-call(s32[1,2]{1,0:T(1,128)S(1)} %copy-done.1, ...), custom_call_target="tpu_custom_call" | custom-call | flops 4294967296 | bytes 14680064 | tf_op jit(solution)/shard_map/probs/pallas_call | solution.py:228
  70.1 2.4 %collective-permute-start.3 = (bf16[1024,128]{1,0:T(8,128)(2,1)}, bf16[1024,128]{1,0:T(8,128)(2,1)}, u32[]{:S(2)}, u32[]{:S(2)}) collective-permute-start(bf16[1024,128]{1,0:T(8,128)(2,1)} %bitcast.18), channel_id=1, source_target_pairs={{0,8},{4,12},{8,0},{12,4},{1,9},{5,13},{9,1},{13,5},{2,10},{6,14},... | collective-permute-start | bytes 786440 | tf_op jit(solution)/shard_map/ppermute | solution.py:420
  72.6 1.2 collective-permute-start.4
  73.7 18.0 %grads.1 = bf16[16,6,128,128]{3,2,1,0:T(8,128)(2,1)} custom-call(s32[1,2]{1,0:T(1,128)S(1)} %copy-done.1, s32[1,32,3]{2,1,0:T(8,128)S(1)} %copy.12.rand_ref, bf16[16,6,128,128]{3,2,1,0:T(8,128)(2,1)S(1)} %bitcast.12, bf16[16,2,128,128]{3,2,1,0:T(8,128)(2,1)} %bitcast.4.v_ref, bf16[16,1024,256]{2,1,0:T(8,128)(2,1)} %get-tuple-element.50.p_hbm, ...), custom_call_target="tpu_custom_call" | custom-call | flops 5368709120 | bytes 14680064 | tf_op jit(solution)/shard_map/grads/pallas_call | solution.py:302
  92.5 4.4 %all-to-all-start.2 = ((bf16[16,768,128]{2,1,0:T(8,128)(2,1)}), bf16[16,768,128]{2,1,0:T(8,128)(2,1)S(1)}, u32[]{:S(2)}, u32[]{:S(2)}) async-start(bf16[16,768,128]{2,1,0:T(8,128)(2,1)} %bitcast.13), calls=%async_computation.2 | async-start | bytes 6291456 | tf_op jit(solution)/shard_map/all_to_all | solution.py:416
  97.1 2.6 %collective-permute-done.5.refs_3_ = bf16[1,256,2048]{2,1,0:T(8,128)(2,1)S(1)} collective-permute-done((bf16[1,256,2048]{2,1,0:T(8,128)(2,1)}, bf16[1,256,2048]{2,1,0:T(8,128)(2,1)S(1)}, u32[]{:S(2)}, u32[]{:S(2)}) %collective-permute-start.5) | collective-permute-done | bytes 1048608 | tf_op jit(solution)/shard_map/ppermute | solution.py:420
  99.7 4.9 %weight.3 = (bf16[256,512]{1,0:T(8,128)(2,1)}, bf16[256,512]{1,0:T(8,128)(2,1)}, bf16[256,512]{1,0:T(8,128)(2,1)}, bf16[256,512]{1,0:T(8,128)(2,1)}) custom-call(s32[3]{0:T(128)S(1)} %pad_add_fusion.me_ref, bf16[1,256,2048]{2,1,0:T(8,128)(2,1)} %refs_0_.3, bf16[1,256,2048]{2,1,0:T(8,128)(2,1)} %collective-permute-done.1.refs_1_, ...), custom_call_target="tpu_custom_call" | custom-call | flops 1073741824 | bytes 4194304 | tf_op jit(solution)/shard_map/weight/pallas_call | solution.py:367
  104.6 2.8 %collective-permute-start.11 = (bf16[256,512]{1,0:T(8,128)(2,1)}, bf16[256,512]{1,0:T(8,128)(2,1)S(1)}, u32[]{:S(2)}, u32[]{:S(2)}) collective-permute-start(bf16[256,512]{1,0:T(8,128)(2,1)} %get-tuple-element.69), channel_id=1, source_target_pairs={{0,96},{32,0},{64,32},{96,64},{1,97},{33,1},{65,33},{97,65},{2,98}... | collective-permute-start | bytes 786440 | tf_op jit(solution)/shard_map/ppermute | solution.py:420
  108.4 4.9 %weight.2 = (bf16[256,512]{1,0:T(8,128)(2,1)}, bf16[256,512]{1,0:T(8,128)(2,1)}, bf16[256,512]{1,0:T(8,128)(2,1)}, bf16[256,512]{1,0:T(8,128)(2,1)}) custom-call(s32[3]{0:T(128)S(1)} %pad_add_fusion.me_ref, bf16[1,256,2048]{2,1,0:T(8,128)(2,1)} %refs_0_.3, bf16[1,256,2048]{2,1,0:T(8,128)(2,1)} %collective-permute-done.1.refs_1_, ...), custom_call_target="tpu_custom_call" | custom-call | flops 1073741824 | bytes 4194304 | tf_op jit(solution)/shard_map/weight/pallas_call | solution.py:367
  113.3 2.2 %collective-permute-start.8 = (bf16[256,512]{1,0:T(8,128)(2,1)}, bf16[256,512]{1,0:T(8,128)(2,1)S(1)}, u32[]{:S(2)}, u32[]{:S(2)}) collective-permute-start(bf16[256,512]{1,0:T(8,128)(2,1)} %get-tuple-element.65), channel_id=1, source_target_pairs={{0,96},{32,0},{64,32},{96,64},{1,97},{33,1},{65,33},{97,65},{2,98}... | collective-permute-start | bytes 786440 | tf_op jit(solution)/shard_map/ppermute | solution.py:420
  115.5 1.3 collective-permute-start.7
  116.8 1.5 collective-permute-done.11
  118.3 5.6 %collective-permute-done.9 = bf16[256,512]{1,0:T(8,128)(2,1)S(1)} collective-permute-done((bf16[256,512]{1,0:T(8,128)(2,1)}, bf16[256,512]{1,0:T(8,128)(2,1)S(1)}, u32[]{:S(2)}, u32[]{:S(2)}) %collective-permute-start.9) | collective-permute-done | bytes 262176 | tf_op jit(solution)/shard_map/ppermute | solution.py:420
  124.0 5.8 %collective-permute-done.8 = bf16[256,512]{1,0:T(8,128)(2,1)S(1)} collective-permute-done((bf16[256,512]{1,0:T(8,128)(2,1)}, bf16[256,512]{1,0:T(8,128)(2,1)S(1)}, u32[]{:S(2)}, u32[]{:S(2)}) %collective-permute-start.8) | collective-permute-done | bytes 262176 | tf_op jit(solution)/shard_map/ppermute | solution.py:420
  129.8 4.3 %collective-permute-done.6 = bf16[256,512]{1,0:T(8,128)(2,1)S(1)} collective-permute-done((bf16[256,512]{1,0:T(8,128)(2,1)}, bf16[256,512]{1,0:T(8,128)(2,1)S(1)}, u32[]{:S(2)}, u32[]{:S(2)}) %collective-permute-start.6) | collective-permute-done | bytes 262176 | tf_op jit(solution)/shard_map/ppermute | solution.py:420
  134.1 1.1 add_convert_fusion.1
  136.3 10.1 %all-to-all-start.3 = ((bf16[32,16,512]{2,1,0:T(8,128)(2,1)}), bf16[32,16,512]{2,1,0:T(8,128)(2,1)}, u32[]{:S(2)}, u32[]{:S(2)}) async-start(bf16[32,16,512]{2,1,0:T(8,128)(2,1)} %bitcast.14), calls=%async_computation.3 | async-start | bytes 1048576 | tf_op jit(solution)/shard_map/all_to_all | solution.py:416
  146.4 2.5 %unpack.1 = (bf16[1,256,2048]{2,1,0:T(8,128)(2,1)}, bf16[1,256,2048]{2,1,0:T(8,128)(2,1)}, bf16[1,256,2048]{2,1,0:T(8,128)(2,1)}) custom-call(bf16[16,768,128]{2,1,0:T(8,128)(2,1)S(1)} %all-to-all-done.2.src), custom_call_target="tpu_custom_call" | custom-call | bytes 6291456 | tf_op jit(solution)/shard_map/unpack/pallas_call | solution.py:92
  149.0 9.3 %all-to-all-done.3.in_ref = bf16[32,16,512]{2,1,0:T(8,128)(2,1)} async-done(((bf16[32,16,512]{2,1,0:T(8,128)(2,1)}), bf16[32,16,512]{2,1,0:T(8,128)(2,1)}, u32[]{:S(2)}, u32[]{:S(2)}) %all-to-all-start.3) | async-done | bytes 524320 | tf_op jit(solution)/shard_map/all_to_all | solution.py:416
  158.2 1.8 %sum.1 = f32[16,2048]{1,0:T(8,128)} custom-call(bf16[32,16,512]{2,1,0:T(8,128)(2,1)} %all-to-all-done.3.in_ref), custom_call_target="tpu_custom_call" | custom-call | flops 262144 | bytes 524288 | tf_op jit(solution)/shard_map/sum/pallas_call | solution.py:403
  (29 shorter events, 5.5 us)
Async XLA Ops:
  3.0 52.2 %copy-start.4 = (s32[1,32,3]{1,0,2:T(1,128)S(1)}, s32[1,32,3]{1,0,2:T(1,128)}, u32[]{:S(2)}) copy-start(s32[1,32,3]{1,0,2:T(1,128)} %param.13) | copy-start | bytes 1156
  3.0 52.4 %copy-start.1 = (s32[1,2]{1,0:T(1,128)S(1)}, s32[1,2]{1,0:T(1,128)}, u32[]{:S(2)}) copy-start(s32[1,2]{1,0:T(1,128)} %glob_ref.3) | copy-start | bytes 28
  47.8 21.3 %all-to-all-start.1 = ((bf16[16,256,128]{2,1,0:T(8,128)(2,1)}), bf16[16,256,128]{2,1,0:T(8,128)(2,1)}, u32[]{:S(2)}, u32[]{:S(2)}) async-start(bf16[16,256,128]{2,1,0:T(8,128)(2,1)} %get-tuple-element.44), calls=%async_computation.1 | async-start | bytes 2097152 | tf_op jit(solution)/shard_map/all_to_all | solution.py:416
  53.2 38.5 %collective-permute-start = (bf16[1,256,2048]{2,1,0:T(8,128)(2,1)}, bf16[1,256,2048]{2,1,0:T(8,128)(2,1)}, u32[]{:S(2)}, u32[]{:S(2)}) collective-permute-start(bf16[1,256,2048]{2,1,0:T(8,128)(2,1)} %refs_0_.3), channel_id=1, source_target_pairs={{0,2},{2,0},{1,3},{3,1},{4,6},{6,4},{5,7},{7,5},{8,10},{10,8},{9,1... | collective-permute-start | bytes 3145736 | tf_op jit(solution)/shard_map/ppermute | solution.py:420
  54.6 37.1 %collective-permute-start.1 = (bf16[1,256,2048]{2,1,0:T(8,128)(2,1)}, bf16[1,256,2048]{2,1,0:T(8,128)(2,1)}, u32[]{:S(2)}, u32[]{:S(2)}) collective-permute-start(bf16[1,256,2048]{2,1,0:T(8,128)(2,1)} %refs_0_.3), channel_id=1, source_target_pairs={{0,1},{1,0},{2,3},{3,2},{4,5},{5,4},{6,7},{7,6},{8,9},{9,8},{10,11... | collective-permute-start | bytes 3145736 | tf_op jit(solution)/shard_map/ppermute | solution.py:420
  55.4 18.3 %copy-start = (bf16[16,768,128]{2,1,0:T(8,128)(2,1)S(1)}, bf16[16,768,128]{2,1,0:T(8,128)(2,1)}, u32[]{:S(2)}) copy-start(bf16[16,768,128]{2,1,0:T(8,128)(2,1)} %all_to_all.20) | copy-start | bytes 9437188
  69.1 22.6 %collective-permute-start.2 = (bf16[1024,128]{1,0:T(8,128)(2,1)}, bf16[1024,128]{1,0:T(8,128)(2,1)S(1)}, u32[]{:S(2)}, u32[]{:S(2)}) collective-permute-start(bf16[1024,128]{1,0:T(8,128)(2,1)} %bitcast.19), channel_id=1, source_target_pairs={{0,4},{4,8},{8,12},{12,0},{1,5},{5,9},{9,13},{13,1},{2,6},{6,10},{... | collective-permute-start | bytes 786440 | tf_op jit(solution)/shard_map/ppermute | solution.py:420
  70.1 21.6 %collective-permute-start.3 = (bf16[1024,128]{1,0:T(8,128)(2,1)}, bf16[1024,128]{1,0:T(8,128)(2,1)}, u32[]{:S(2)}, u32[]{:S(2)}) collective-permute-start(bf16[1024,128]{1,0:T(8,128)(2,1)} %bitcast.18), channel_id=1, source_target_pairs={{0,8},{4,12},{8,0},{12,4},{1,9},{5,13},{9,1},{13,5},{2,10},{6,14},... | collective-permute-start | bytes 786440 | tf_op jit(solution)/shard_map/ppermute | solution.py:420
  72.6 19.2 %collective-permute-start.4 = (bf16[1024,128]{1,0:T(8,128)(2,1)}, bf16[1024,128]{1,0:T(8,128)(2,1)}, u32[]{:S(2)}, u32[]{:S(2)}) collective-permute-start(bf16[1024,128]{1,0:T(8,128)(2,1)} %bitcast.17), channel_id=1, source_target_pairs={{0,12},{4,0},{8,4},{12,8},{1,13},{5,1},{9,5},{13,9},{2,14},{6,2},{... | collective-permute-start | bytes 786440 | tf_op jit(solution)/shard_map/ppermute | solution.py:420
  91.7 0.7 copy-start.2
  92.5 43.9 %all-to-all-start.2 = ((bf16[16,768,128]{2,1,0:T(8,128)(2,1)}), bf16[16,768,128]{2,1,0:T(8,128)(2,1)S(1)}, u32[]{:S(2)}, u32[]{:S(2)}) async-start(bf16[16,768,128]{2,1,0:T(8,128)(2,1)} %bitcast.13), calls=%async_computation.2 | async-start | bytes 6291456 | tf_op jit(solution)/shard_map/all_to_all | solution.py:416
  96.8 2.9 %collective-permute-start.5 = (bf16[1,256,2048]{2,1,0:T(8,128)(2,1)}, bf16[1,256,2048]{2,1,0:T(8,128)(2,1)S(1)}, u32[]{:S(2)}, u32[]{:S(2)}) collective-permute-start(bf16[1,256,2048]{2,1,0:T(8,128)(2,1)} %collective-permute-done.refs_2_), channel_id=1, source_target_pairs={{0,1},{1,0},{2,3},{3,2},{4,5},{5,4},{6,7},{7,6},{8,9},{9,8},{10,11... | collective-permute-start | bytes 3145736 | tf_op jit(solution)/shard_map/ppermute | solution.py:420
  104.6 19.3 %copy-start.3 = (bf16[256,512]{1,0:T(8,128)(2,1)S(1)}, bf16[256,512]{1,0:T(8,128)(2,1)}, u32[]{:S(2)}) copy-start(bf16[256,512]{1,0:T(8,128)(2,1)} %get-tuple-element.66) | copy-start | bytes 786436
  104.6 13.7 %collective-permute-start.11 = (bf16[256,512]{1,0:T(8,128)(2,1)}, bf16[256,512]{1,0:T(8,128)(2,1)S(1)}, u32[]{:S(2)}, u32[]{:S(2)}) collective-permute-start(bf16[256,512]{1,0:T(8,128)(2,1)} %get-tuple-element.69), channel_id=1, source_target_pairs={{0,96},{32,0},{64,32},{96,64},{1,97},{33,1},{65,33},{97,65},{2,98}... | collective-permute-start | bytes 786440 | tf_op jit(solution)/shard_map/ppermute | solution.py:420
  107.4 10.9 %collective-permute-start.10 = (bf16[256,512]{1,0:T(8,128)(2,1)}, bf16[256,512]{1,0:T(8,128)(2,1)S(1)}, u32[]{:S(2)}, u32[]{:S(2)}) collective-permute-start(bf16[256,512]{1,0:T(8,128)(2,1)} %get-tuple-element.68), channel_id=1, source_target_pairs={{0,64},{32,96},{64,0},{96,32},{1,65},{33,97},{65,1},{97,33},{2,66}... | collective-permute-start | bytes 786440 | tf_op jit(solution)/shard_map/ppermute | solution.py:420
  107.9 16.0 %collective-permute-start.9 = (bf16[256,512]{1,0:T(8,128)(2,1)}, bf16[256,512]{1,0:T(8,128)(2,1)S(1)}, u32[]{:S(2)}, u32[]{:S(2)}) collective-permute-start(bf16[256,512]{1,0:T(8,128)(2,1)} %get-tuple-element.67), channel_id=1, source_target_pairs={{0,32},{32,64},{64,96},{96,0},{1,33},{33,65},{65,97},{97,1},{2,34}... | collective-permute-start | bytes 786440 | tf_op jit(solution)/shard_map/ppermute | solution.py:420
  113.3 16.5 %collective-permute-start.8 = (bf16[256,512]{1,0:T(8,128)(2,1)}, bf16[256,512]{1,0:T(8,128)(2,1)S(1)}, u32[]{:S(2)}, u32[]{:S(2)}) collective-permute-start(bf16[256,512]{1,0:T(8,128)(2,1)} %get-tuple-element.65), channel_id=1, source_target_pairs={{0,96},{32,0},{64,32},{96,64},{1,97},{33,1},{65,33},{97,65},{2,98}... | collective-permute-start | bytes 786440 | tf_op jit(solution)/shard_map/ppermute | solution.py:420
  115.5 14.3 %collective-permute-start.7 = (bf16[256,512]{1,0:T(8,128)(2,1)}, bf16[256,512]{1,0:T(8,128)(2,1)S(1)}, u32[]{:S(2)}, u32[]{:S(2)}) collective-permute-start(bf16[256,512]{1,0:T(8,128)(2,1)} %get-tuple-element.64), channel_id=1, source_target_pairs={{0,64},{32,96},{64,0},{96,32},{1,65},{33,97},{65,1},{97,33},{2,66}... | collective-permute-start | bytes 786440 | tf_op jit(solution)/shard_map/ppermute | solution.py:420
  118.3 15.8 %collective-permute-start.6 = (bf16[256,512]{1,0:T(8,128)(2,1)}, bf16[256,512]{1,0:T(8,128)(2,1)S(1)}, u32[]{:S(2)}, u32[]{:S(2)}) collective-permute-start(bf16[256,512]{1,0:T(8,128)(2,1)} %get-tuple-element.63), channel_id=1, source_target_pairs={{0,32},{32,64},{64,96},{96,0},{1,33},{33,65},{65,97},{97,1},{2,34}... | collective-permute-start | bytes 786440 | tf_op jit(solution)/shard_map/ppermute | solution.py:420
  136.3 21.9 %all-to-all-start.3 = ((bf16[32,16,512]{2,1,0:T(8,128)(2,1)}), bf16[32,16,512]{2,1,0:T(8,128)(2,1)}, u32[]{:S(2)}, u32[]{:S(2)}) async-start(bf16[32,16,512]{2,1,0:T(8,128)(2,1)} %bitcast.14), calls=%async_computation.3 | async-start | bytes 1048576 | tf_op jit(solution)/shard_map/all_to_all | solution.py:416

commit v5 on v4

--- a/solution.py
+++ b/solution.py
@@ -258,11 +258,12 @@
     def load(u):
         return pltpu.make_async_copy(p_hbm.at[u], p_ref.at[u], sems.at[u])
 
-    for u in range(half_nb):
+    quarter = half_nb // 4
+    for u in range(quarter):
         load(u).start()
     dv_load = pltpu.make_async_copy(dv_hbm, out_ref.at[:, pl.ds(2 * DV, 2)], sems.at[half_nb])
-    dv_load.start()
     acc[...] = jnp.zeros_like(acc)
+
     def pair(u):
         idx_pair = [table_row(glob_ref, rand_ref, 2 * u + half, nb)[0] for half in range(2)]
         vals = jnp.concatenate([pick(v_ref, idx, 0) for idx in idx_pair], axis=1)
@@ -279,19 +280,18 @@
         part = jnp.dot(ds, two(in_ref, u, Q), preferred_element_type=F32)
         add_tiles(acc, idx_pair, part)
 
-    quarter = half_nb // 4
-
-    def batch(first, size):
+    def batch(first, size, after):
         for u in range(size):
             load(first + u).wait()
+        for u in range(after):
+            load(first + size + u).start()
         for u in range(size):
             pair(first + u)
 
-    @pl.loop(0, 2)
-    def _(step):
-        batch(step * quarter, quarter)
-
-    batch(2 * quarter, 2 * quarter)
+    batch(0, quarter, 3 * quarter)
+    dv_load.start()
+    batch(quarter, 3 * quarter, 0)
+
     out_ref[:, 2 * DK : 2 * DK + 2] = (acc[...] * scale).astype(BF16).reshape(dv_hbm.shape)
     dv_load.wait()
 
@@ -447,7 +447,7 @@
     back = swap(qkv.reshape(n_ctx, 3 * local, D), CTX)
     x_both = vmem_pin(shift(x_zl, "core", 1, 2))
     xs = [hbm(x_own), hbm(x_core), hbm(x_zl), x_both]
-    parts = [hbm(part) for part in parts]
+    parts = [vmem_pin(part) if n == 1 else hbm(part) for n, part in enumerate(parts)]
     w_y = []
     for half in range(2):
         tiles = weight_call(me, xs, parts, nz, ny, half)

time: 161 us -> 160 us (level)
  no operation moved by 1% of the time
where the time goes in v5:
time: 160 us; the launch traced here: 159 us
  Pallas kernels  47.2 us (30%)
  blocking collectives  44.8 us (28%)
  starting transfers between devices  34.2 us (21%)
  waiting for transfers between devices  29.8 us (19%)
  other arithmetic  2.13 us (1%)
    all_to_all x1, blocking collectives, swap(): return lax.all_to_all(array, axes, split_axis=0, concat_axis=0, tiled=True)  44.8 us
    all_to_all x3, starting transfers between devices, swap(): return lax.all_to_all(array, axes, split_axis=0, concat_axis=0, tiled=True)  19.9 us
    ppermute x12, waiting for transfers between devices, shift(): return lax.ppermute(array, axis, [(i, (i + n) % size) for i in range(size)])  19.8 us
    pallas_call x1, Pallas kernels, grads_call(): pl.pallas_call(functools.partial(grads_kernel, scale), out_shape=pltpu.HB...  17.6 us
    ppermute x12, starting transfers between devices, shift(): return lax.ppermute(array, axis, [(i, (i + n) % size) for i in range(size)])  14.3 us
    pallas_call x1, Pallas kernels, probs_call(): pl.pallas_call(functools.partial(probs_kernel, nx, scale), out_shape=[plt...  13.4 us
    all_to_all x3, waiting for transfers between devices, swap(): return lax.all_to_all(array, axes, split_axis=0, concat_axis=0, tiled=True)  9.93 us
    pallas_call x2, Pallas kernels, weight_call(): pl.pallas_call(functools.partial(weight_kernel, len(xs), nx, nz, ny, half...  9.59 us
  transfers between devices with their start and end apart: 15, of which 8 were waited for; matrix products, arithmetic and copies ran while one was open for 1% of the time, Pallas kernels for 27%

profile of v5, /device:TPU:1, one launch (start us, length us, event | category | flops | bytes accessed | tf_op | source)
XLA Modules:
  0.0 158.9 jit_solution(707355107696041673)
XLA Ops:
  0.6 2.4 %pack.1 = (bf16[16,768,128]{2,1,0:T(8,128)(2,1)S(1)}, bf16[16,256,128]{2,1,0:T(8,128)(2,1)}) custom-call(bf16[1,256,2048]{2,1,0:T(8,128)(2,1)} %refs_0_.1, bf16[1,256,2048]{2,1,0:T(8,128)(2,1)} %refs_1_.1, bf16[1,256,2048]{2,1,0:T(8,128)(2,1)} %refs_2_.1, bf16[1,256,2048]{2,1,0:T(8,128)(2,1)} %refs_3_.1), custom_call_target="tpu_custom_call" | custom-call | bytes 8388608 | tf_op jit(solution)/shard_map/pack/pallas_call | solution.py:61
  3.0 44.8 %all_to_all.20 = bf16[16,768,128]{2,1,0:T(8,128)(2,1)} all-to-all(bf16[16,768,128]{2,1,0:T(8,128)(2,1)S(1)} %get-tuple-element.40), channel_id=1, replica_groups=mesh['y'=4,'zh'=2,'x'=4,'zl'=2,'core'=2] {'x','zl','core'}, dimensions={0} | all-to-all | bytes 6291456 | tf_op jit(solution)/shard_map/all_to_all | solution.py:416
  47.8 5.4 %all-to-all-start.1 = ((bf16[16,256,128]{2,1,0:T(8,128)(2,1)}), bf16[16,256,128]{2,1,0:T(8,128)(2,1)}, u32[]{:S(2)}, u32[]{:S(2)}) async-start(bf16[16,256,128]{2,1,0:T(8,128)(2,1)} %get-tuple-element.44), calls=%async_computation.1 | async-start | bytes 2097152 | tf_op jit(solution)/shard_map/all_to_all | solution.py:416
  53.2 1.4 collective-permute-start
  55.4 13.4 %probs.1 = (bf16[16,1024,256]{2,1,0:T(8,128)(2,1)}, bf16[16,2,128,128]{3,2,1,0:T(8,128)(2,1)}, bf16[4,2,128,128]{3,2,1,0:T(8,128)(2,1)}, bf16[4,2,128,128]{3,2,1...) custom-call(s32[1,2]{1,0:T(1,128)S(1)} %copy-done.1, ...), custom_call_target="tpu_custom_call" | custom-call | flops 4294967296 | bytes 14680064 | tf_op jit(solution)/shard_map/probs/pallas_call | solution.py:228
  70.1 2.5 %collective-permute-start.3 = (bf16[1024,128]{1,0:T(8,128)(2,1)}, bf16[1024,128]{1,0:T(8,128)(2,1)}, u32[]{:S(2)}, u32[]{:S(2)}) collective-permute-start(bf16[1024,128]{1,0:T(8,128)(2,1)} %bitcast.18), channel_id=1, source_target_pairs={{0,8},{4,12},{8,0},{12,4},{1,9},{5,13},{9,1},{13,5},{2,10},{6,14},... | collective-permute-start | bytes 786440 | tf_op jit(solution)/shard_map/ppermute | solution.py:420
  72.6 1.2 collective-permute-start.4
  73.7 17.6 %grads.1 = bf16[16,6,128,128]{3,2,1,0:T(8,128)(2,1)} custom-call(s32[1,2]{1,0:T(1,128)S(1)} %copy-done.1, s32[1,32,3]{2,1,0:T(8,128)S(1)} %copy.12.rand_ref, bf16[16,6,128,128]{3,2,1,0:T(8,128)(2,1)S(1)} %bitcast.12, bf16[16,2,128,128]{3,2,1,0:T(8,128)(2,1)} %bitcast.4.v_ref, bf16[16,1024,256]{2,1,0:T(8,128)(2,1)} %get-tuple-element.50.p_hbm, ...), custom_call_target="tpu_custom_call" | custom-call | flops 5368709120 | bytes 14680064 | tf_op jit(solution)/shard_map/grads/pallas_call | solution.py:302
  91.4 4.4 %all-to-all-start.2 = ((bf16[16,768,128]{2,1,0:T(8,128)(2,1)}), bf16[16,768,128]{2,1,0:T(8,128)(2,1)S(1)}, u32[]{:S(2)}, u32[]{:S(2)}) async-start(bf16[16,768,128]{2,1,0:T(8,128)(2,1)} %bitcast.13), calls=%async_computation.2 | async-start | bytes 6291456 | tf_op jit(solution)/shard_map/all_to_all | solution.py:416
  96.1 2.6 %collective-permute-done.5.refs_3_ = bf16[1,256,2048]{2,1,0:T(8,128)(2,1)S(1)} collective-permute-done((bf16[1,256,2048]{2,1,0:T(8,128)(2,1)}, bf16[1,256,2048]{2,1,0:T(8,128)(2,1)S(1)}, u32[]{:S(2)}, u32[]{:S(2)}) %collective-permute-start.5) | collective-permute-done | bytes 1048608 | tf_op jit(solution)/shard_map/ppermute | solution.py:420
  98.6 4.8 %weight.3 = (bf16[256,512]{1,0:T(8,128)(2,1)}, bf16[256,512]{1,0:T(8,128)(2,1)}, bf16[256,512]{1,0:T(8,128)(2,1)}, bf16[256,512]{1,0:T(8,128)(2,1)}) custom-call(s32[3]{0:T(128)S(1)} %pad_add_fusion.me_ref, bf16[1,256,2048]{2,1,0:T(8,128)(2,1)} %refs_0_.3, bf16[1,256,2048]{2,1,0:T(8,128)(2,1)} %collective-permute-done.1.refs_1_, ...), custom_call_target="tpu_custom_call" | custom-call | flops 1073741824 | bytes 4194304 | tf_op jit(solution)/shard_map/weight/pallas_call | solution.py:367
  103.5 2.8 %collective-permute-start.11 = (bf16[256,512]{1,0:T(8,128)(2,1)}, bf16[256,512]{1,0:T(8,128)(2,1)S(1)}, u32[]{:S(2)}, u32[]{:S(2)}) collective-permute-start(bf16[256,512]{1,0:T(8,128)(2,1)} %get-tuple-element.69), channel_id=1, source_target_pairs={{0,96},{32,0},{64,32},{96,64},{1,97},{33,1},{65,33},{97,65},{2,98}... | collective-permute-start | bytes 786440 | tf_op jit(solution)/shard_map/ppermute | solution.py:420
  107.3 4.8 %weight.2 = (bf16[256,512]{1,0:T(8,128)(2,1)}, bf16[256,512]{1,0:T(8,128)(2,1)}, bf16[256,512]{1,0:T(8,128)(2,1)}, bf16[256,512]{1,0:T(8,128)(2,1)}) custom-call(s32[3]{0:T(128)S(1)} %pad_add_fusion.me_ref, bf16[1,256,2048]{2,1,0:T(8,128)(2,1)} %refs_0_.3, bf16[1,256,2048]{2,1,0:T(8,128)(2,1)} %collective-permute-done.1.refs_1_, ...), custom_call_target="tpu_custom_call" | custom-call | flops 1073741824 | bytes 4194304 | tf_op jit(solution)/shard_map/weight/pallas_call | solution.py:367
  112.1 2.1 %collective-permute-start.8 = (bf16[256,512]{1,0:T(8,128)(2,1)}, bf16[256,512]{1,0:T(8,128)(2,1)S(1)}, u32[]{:S(2)}, u32[]{:S(2)}) collective-permute-start(bf16[256,512]{1,0:T(8,128)(2,1)} %get-tuple-element.65), channel_id=1, source_target_pairs={{0,96},{32,0},{64,32},{96,64},{1,97},{33,1},{65,33},{97,65},{2,98}... | collective-permute-start | bytes 786440 | tf_op jit(solution)/shard_map/ppermute | solution.py:420
  114.2 1.4 collective-permute-start.7
  115.6 1.6 collective-permute-done.11
  117.1 5.6 %collective-permute-done.9 = bf16[256,512]{1,0:T(8,128)(2,1)S(1)} collective-permute-done((bf16[256,512]{1,0:T(8,128)(2,1)}, bf16[256,512]{1,0:T(8,128)(2,1)S(1)}, u32[]{:S(2)}, u32[]{:S(2)}) %collective-permute-start.9) | collective-permute-done | bytes 262176 | tf_op jit(solution)/shard_map/ppermute | solution.py:420
  122.9 5.8 %collective-permute-done.8 = bf16[256,512]{1,0:T(8,128)(2,1)S(1)} collective-permute-done((bf16[256,512]{1,0:T(8,128)(2,1)}, bf16[256,512]{1,0:T(8,128)(2,1)S(1)}, u32[]{:S(2)}, u32[]{:S(2)}) %collective-permute-start.8) | collective-permute-done | bytes 262176 | tf_op jit(solution)/shard_map/ppermute | solution.py:420
  128.7 4.3 %collective-permute-done.6 = bf16[256,512]{1,0:T(8,128)(2,1)S(1)} collective-permute-done((bf16[256,512]{1,0:T(8,128)(2,1)}, bf16[256,512]{1,0:T(8,128)(2,1)S(1)}, u32[]{:S(2)}, u32[]{:S(2)}) %collective-permute-start.6) | collective-permute-done | bytes 262176 | tf_op jit(solution)/shard_map/ppermute | solution.py:420
  133.0 1.1 add_convert_fusion.1
  135.3 10.1 %all-to-all-start.3 = ((bf16[32,16,512]{2,1,0:T(8,128)(2,1)}), bf16[32,16,512]{2,1,0:T(8,128)(2,1)}, u32[]{:S(2)}, u32[]{:S(2)}) async-start(bf16[32,16,512]{2,1,0:T(8,128)(2,1)} %bitcast.14), calls=%async_computation.3 | async-start | bytes 1048576 | tf_op jit(solution)/shard_map/all_to_all | solution.py:416
  145.4 2.5 %unpack.1 = (bf16[1,256,2048]{2,1,0:T(8,128)(2,1)}, bf16[1,256,2048]{2,1,0:T(8,128)(2,1)}, bf16[1,256,2048]{2,1,0:T(8,128)(2,1)}) custom-call(bf16[16,768,128]{2,1,0:T(8,128)(2,1)S(1)} %all-to-all-done.2.src), custom_call_target="tpu_custom_call" | custom-call | bytes 6291456 | tf_op jit(solution)/shard_map/unpack/pallas_call | solution.py:92
  147.9 9.3 %all-to-all-done.3.in_ref = bf16[32,16,512]{2,1,0:T(8,128)(2,1)} async-done(((bf16[32,16,512]{2,1,0:T(8,128)(2,1)}), bf16[32,16,512]{2,1,0:T(8,128)(2,1)}, u32[]{:S(2)}, u32[]{:S(2)}) %all-to-all-start.3) | async-done | bytes 524320 | tf_op jit(solution)/shard_map/all_to_all | solution.py:416
  157.2 1.8 %sum.1 = f32[16,2048]{1,0:T(8,128)} custom-call(bf16[32,16,512]{2,1,0:T(8,128)(2,1)} %all-to-all-done.3.in_ref), custom_call_target="tpu_custom_call" | custom-call | flops 262144 | bytes 524288 | tf_op jit(solution)/shard_map/sum/pallas_call | solution.py:403
  (27 shorter events, 4.9 us)
Async XLA Ops:
  3.0 52.3 %copy-start.3 = (s32[1,32,3]{1,0,2:T(1,128)S(1)}, s32[1,32,3]{1,0,2:T(1,128)}, u32[]{:S(2)}) copy-start(s32[1,32,3]{1,0,2:T(1,128)} %param.13) | copy-start | bytes 1156
  3.0 52.4 %copy-start.1 = (s32[1,2]{1,0:T(1,128)S(1)}, s32[1,2]{1,0:T(1,128)}, u32[]{:S(2)}) copy-start(s32[1,2]{1,0:T(1,128)} %glob_ref.3) | copy-start | bytes 28
  47.8 21.3 %all-to-all-start.1 = ((bf16[16,256,128]{2,1,0:T(8,128)(2,1)}), bf16[16,256,128]{2,1,0:T(8,128)(2,1)}, u32[]{:S(2)}, u32[]{:S(2)}) async-start(bf16[16,256,128]{2,1,0:T(8,128)(2,1)} %get-tuple-element.44), calls=%async_computation.1 | async-start | bytes 2097152 | tf_op jit(solution)/shard_map/all_to_all | solution.py:416
  53.2 38.1 %collective-permute-start = (bf16[1,256,2048]{2,1,0:T(8,128)(2,1)}, bf16[1,256,2048]{2,1,0:T(8,128)(2,1)}, u32[]{:S(2)}, u32[]{:S(2)}) collective-permute-start(bf16[1,256,2048]{2,1,0:T(8,128)(2,1)} %refs_0_.3), channel_id=1, source_target_pairs={{0,2},{2,0},{1,3},{3,1},{4,6},{6,4},{5,7},{7,5},{8,10},{10,8},{9,1... | collective-permute-start | bytes 3145736 | tf_op jit(solution)/shard_map/ppermute | solution.py:420
  54.6 36.7 %collective-permute-start.1 = (bf16[1,256,2048]{2,1,0:T(8,128)(2,1)}, bf16[1,256,2048]{2,1,0:T(8,128)(2,1)}, u32[]{:S(2)}, u32[]{:S(2)}) collective-permute-start(bf16[1,256,2048]{2,1,0:T(8,128)(2,1)} %refs_0_.3), channel_id=1, source_target_pairs={{0,1},{1,0},{2,3},{3,2},{4,5},{5,4},{6,7},{7,6},{8,9},{9,8},{10,11... | collective-permute-start | bytes 3145736 | tf_op jit(solution)/shard_map/ppermute | solution.py:420
  55.4 18.3 %copy-start = (bf16[16,768,128]{2,1,0:T(8,128)(2,1)S(1)}, bf16[16,768,128]{2,1,0:T(8,128)(2,1)}, u32[]{:S(2)}) copy-start(bf16[16,768,128]{2,1,0:T(8,128)(2,1)} %all_to_all.20) | copy-start | bytes 9437188
  69.1 22.2 %collective-permute-start.2 = (bf16[1024,128]{1,0:T(8,128)(2,1)}, bf16[1024,128]{1,0:T(8,128)(2,1)S(1)}, u32[]{:S(2)}, u32[]{:S(2)}) collective-permute-start(bf16[1024,128]{1,0:T(8,128)(2,1)} %bitcast.19), channel_id=1, source_target_pairs={{0,4},{4,8},{8,12},{12,0},{1,5},{5,9},{9,13},{13,1},{2,6},{6,10},{... | collective-permute-start | bytes 786440 | tf_op jit(solution)/shard_map/ppermute | solution.py:420
  70.1 21.2 %collective-permute-start.3 = (bf16[1024,128]{1,0:T(8,128)(2,1)}, bf16[1024,128]{1,0:T(8,128)(2,1)}, u32[]{:S(2)}, u32[]{:S(2)}) collective-permute-start(bf16[1024,128]{1,0:T(8,128)(2,1)} %bitcast.18), channel_id=1, source_target_pairs={{0,8},{4,12},{8,0},{12,4},{1,9},{5,13},{9,1},{13,5},{2,10},{6,14},... | collective-permute-start | bytes 786440 | tf_op jit(solution)/shard_map/ppermute | solution.py:420
  72.6 18.8 %collective-permute-start.4 = (bf16[1024,128]{1,0:T(8,128)(2,1)}, bf16[1024,128]{1,0:T(8,128)(2,1)}, u32[]{:S(2)}, u32[]{:S(2)}) collective-permute-start(bf16[1024,128]{1,0:T(8,128)(2,1)} %bitcast.17), channel_id=1, source_target_pairs={{0,12},{4,0},{8,4},{12,8},{1,13},{5,1},{9,5},{13,9},{2,14},{6,2},{... | collective-permute-start | bytes 786440 | tf_op jit(solution)/shard_map/ppermute | solution.py:420
  91.4 43.9 %all-to-all-start.2 = ((bf16[16,768,128]{2,1,0:T(8,128)(2,1)}), bf16[16,768,128]{2,1,0:T(8,128)(2,1)S(1)}, u32[]{:S(2)}, u32[]{:S(2)}) async-start(bf16[16,768,128]{2,1,0:T(8,128)(2,1)} %bitcast.13), calls=%async_computation.2 | async-start | bytes 6291456 | tf_op jit(solution)/shard_map/all_to_all | solution.py:416
  95.8 2.9 %collective-permute-start.5 = (bf16[1,256,2048]{2,1,0:T(8,128)(2,1)}, bf16[1,256,2048]{2,1,0:T(8,128)(2,1)S(1)}, u32[]{:S(2)}, u32[]{:S(2)}) collective-permute-start(bf16[1,256,2048]{2,1,0:T(8,128)(2,1)} %collective-permute-done.refs_2_), channel_id=1, source_target_pairs={{0,1},{1,0},{2,3},{3,2},{4,5},{5,4},{6,7},{7,6},{8,9},{9,8},{10,11... | collective-permute-start | bytes 3145736 | tf_op jit(solution)/shard_map/ppermute | solution.py:420
  103.5 19.3 %copy-start.2 = (bf16[256,512]{1,0:T(8,128)(2,1)S(1)}, bf16[256,512]{1,0:T(8,128)(2,1)}, u32[]{:S(2)}) copy-start(bf16[256,512]{1,0:T(8,128)(2,1)} %get-tuple-element.66) | copy-start | bytes 786436
  103.5 13.7 %collective-permute-start.11 = (bf16[256,512]{1,0:T(8,128)(2,1)}, bf16[256,512]{1,0:T(8,128)(2,1)S(1)}, u32[]{:S(2)}, u32[]{:S(2)}) collective-permute-start(bf16[256,512]{1,0:T(8,128)(2,1)} %get-tuple-element.69), channel_id=1, source_target_pairs={{0,96},{32,0},{64,32},{96,64},{1,97},{33,1},{65,33},{97,65},{2,98}... | collective-permute-start | bytes 786440 | tf_op jit(solution)/shard_map/ppermute | solution.py:420
  106.3 10.9 %collective-permute-start.10 = (bf16[256,512]{1,0:T(8,128)(2,1)}, bf16[256,512]{1,0:T(8,128)(2,1)S(1)}, u32[]{:S(2)}, u32[]{:S(2)}) collective-permute-start(bf16[256,512]{1,0:T(8,128)(2,1)} %get-tuple-element.68), channel_id=1, source_target_pairs={{0,64},{32,96},{64,0},{96,32},{1,65},{33,97},{65,1},{97,33},{2,66}... | collective-permute-start | bytes 786440 | tf_op jit(solution)/shard_map/ppermute | solution.py:420
  106.6 16.1 %collective-permute-start.9 = (bf16[256,512]{1,0:T(8,128)(2,1)}, bf16[256,512]{1,0:T(8,128)(2,1)S(1)}, u32[]{:S(2)}, u32[]{:S(2)}) collective-permute-start(bf16[256,512]{1,0:T(8,128)(2,1)} %get-tuple-element.67), channel_id=1, source_target_pairs={{0,32},{32,64},{64,96},{96,0},{1,33},{33,65},{65,97},{97,1},{2,34}... | collective-permute-start | bytes 786440 | tf_op jit(solution)/shard_map/ppermute | solution.py:420
  112.1 16.6 %collective-permute-start.8 = (bf16[256,512]{1,0:T(8,128)(2,1)}, bf16[256,512]{1,0:T(8,128)(2,1)S(1)}, u32[]{:S(2)}, u32[]{:S(2)}) collective-permute-start(bf16[256,512]{1,0:T(8,128)(2,1)} %get-tuple-element.65), channel_id=1, source_target_pairs={{0,96},{32,0},{64,32},{96,64},{1,97},{33,1},{65,33},{97,65},{2,98}... | collective-permute-start | bytes 786440 | tf_op jit(solution)/shard_map/ppermute | solution.py:420
  114.2 14.5 %collective-permute-start.7 = (bf16[256,512]{1,0:T(8,128)(2,1)}, bf16[256,512]{1,0:T(8,128)(2,1)S(1)}, u32[]{:S(2)}, u32[]{:S(2)}) collective-permute-start(bf16[256,512]{1,0:T(8,128)(2,1)} %get-tuple-element.64), channel_id=1, source_target_pairs={{0,64},{32,96},{64,0},{96,32},{1,65},{33,97},{65,1},{97,33},{2,66}... | collective-permute-start | bytes 786440 | tf_op jit(solution)/shard_map/ppermute | solution.py:420
  117.1 15.8 %collective-permute-start.6 = (bf16[256,512]{1,0:T(8,128)(2,1)}, bf16[256,512]{1,0:T(8,128)(2,1)S(1)}, u32[]{:S(2)}, u32[]{:S(2)}) collective-permute-start(bf16[256,512]{1,0:T(8,128)(2,1)} %get-tuple-element.63), channel_id=1, source_target_pairs={{0,32},{32,64},{64,96},{96,0},{1,33},{33,65},{65,97},{97,1},{2,34}... | collective-permute-start | bytes 786440 | tf_op jit(solution)/shard_map/ppermute | solution.py:420
  135.3 21.9 %all-to-all-start.3 = ((bf16[32,16,512]{2,1,0:T(8,128)(2,1)}), bf16[32,16,512]{2,1,0:T(8,128)(2,1)}, u32[]{:S(2)}, u32[]{:S(2)}) async-start(bf16[32,16,512]{2,1,0:T(8,128)(2,1)} %bitcast.14), calls=%async_computation.3 | async-start | bytes 1048576 | tf_op jit(solution)/shard_map/all_to_all | solution.py:416
